TPU v7x, 128 devices: a whole 4x4x4 slice. The times are simulated.
128 devices in a mesh: gx: 16 (over z, y), gy: 8 (over x, core).
Axes of the slice: x: 4, y: 4, z: 4, core: 2. Of those that a mesh axis runs over, the one named last changes fastest.
Arguments:
- fractions: float32 [16384, 3, 128], P(('gx', 'gy')), may hold values from 0 to 1
- normals: float32 [16384, 3, 128], P(('gx', 'gy')), may hold values from -6 to 6
- point_cells: int32 [16384, 128], P(('gx', 'gy')), may hold values from 0 to 1574
- block_owner: int32 [16384, 1], P(('gx', 'gy')), may hold values from 0 to 127; in each aligned block of 128 rows (0 to 127, 128 to 255, ...) at most 2 rows name the same one
- block_tile: int32 [16384], P(('gx', 'gy')), may hold values from 0 to 127
- block_count: int32 [16384], P(('gx', 'gy')), may hold values from 1 to 128
Outputs:
- solution_field: float32 [16, 1024, 2048], P(None, 'gx', 'gy')
- residual: float32 [16, 1024, 2048], P(None, 'gx', 'gy')
Inputs may be any that keep to these rules, and one draw needn't show every extreme that they name: `block_owner`: among the blocks of one device, no owner is named by more than 2 blocks.
All inputs are finite; a program needn't handle non-finite values.
Results may differ from a plain program's by a relative error of at most 0.0003.
Values sent between devices are 32-bit elements; how exact they have to be, the bound alone decides.
A program may use at most 128 MiB of HBM per device.

v0:
```python
import jax
import jax.numpy as jnp
from jax import lax
from jax.sharding import PartitionSpec as P

CX = 64
CY = 256
CZ = 16
TX = 8
TY = 16
ITERS = 3


screen_weight = 4.0


def with_halo(block, sides, width):
    for axis, dim in sides:
        count = lax.axis_size(axis)
        forward = [(i, i + 1) for i in range(count - 1)]
        backward = [(target, source) for source, target in forward]
        low = lax.ppermute(
            lax.slice_in_dim(block, block.shape[dim] - width, None, axis=dim), axis, forward
        )
        high = lax.ppermute(lax.slice_in_dim(block, 0, width, axis=dim), axis, backward)
        block = jnp.concatenate([low, block, high], axis=dim)
    return block


def spline_taps(anchor, offsets, length):
    places = jnp.arange(length, dtype=jnp.int32)
    lower = (places[None, :] == anchor[:, None]).astype(jnp.float32)
    upper = (places[None, :] == anchor[:, None] + 1).astype(jnp.float32)
    return (lower * (1.0 - offsets[:, None]) + upper * offsets[:, None], upper - lower)


def splat_block(fractions, normals, cells, count):
    points = cells.shape[0]
    valid = (jnp.arange(points, dtype=jnp.int32) < count).astype(jnp.float32)
    plane = cells % (CZ - 1)
    remains = cells // (CZ - 1)
    column = remains % (TY - 1)
    row_index = remains // (TY - 1)
    weight_x, slope_x = spline_taps(row_index, fractions[0], TX)
    weight_y, slope_y = spline_taps(column, fractions[1], TY)
    weight_z, slope_z = spline_taps(plane, fractions[2], CZ)

    def outer_pair(first, second):
        return (first[:, :, None] * second[:, None, :]).reshape(points, CZ * TX)

    shared = outer_pair(weight_z, weight_x)
    left = jnp.concatenate(
        [
            (normals[0] * valid)[:, None] * outer_pair(weight_z, slope_x),
            (normals[1] * valid)[:, None] * shared,
            (normals[2] * valid)[:, None] * outer_pair(slope_z, weight_x),
        ],
        axis=0,
    )
    right = jnp.concatenate([weight_y, slope_y, weight_y], axis=0)
    source = jnp.dot(
        left.T, right, precision=lax.Precision.HIGHEST, preferred_element_type=jnp.float32
    )
    density = jnp.dot(
        (valid[:, None] * shared).T,
        weight_y,
        precision=lax.Precision.HIGHEST,
        preferred_element_type=jnp.float32,
    )
    return jnp.stack([source, density])


def splat_many(fractions, normals, cells, counts):
    return lax.map(
        lambda items: splat_block(*items), (fractions, normals, cells, counts), batch_size=128
    )


def assemble(tiles, tile_ids):
    tiles_x = CX // TX
    tiles_y = CY // TY
    flat = tiles.reshape((-1, 2, CZ * TX, TY))
    summed = jax.ops.segment_sum(flat, tile_ids.reshape(-1), num_segments=tiles_x * tiles_y)
    fields = summed.reshape(tiles_x, tiles_y, 2, CZ, TX, TY)
    return fields.transpose(2, 3, 0, 4, 1, 5).reshape(2, CZ, CX, CY)


def box_sum(padded):
    total = padded[:-2] + padded[1:-1] + padded[2:]
    total = total[:, :-2] + total[:, 1:-1] + total[:, 2:]
    return total[:, :, :-2] + total[:, :, 1:-1] + total[:, :, 2:]


def operate(field, diagonal):
    widened = with_halo(field, (("gx", 1), ("gy", 2)), 1)
    padded = jnp.pad(widened, ((1, 1), (0, 0), (0, 0)))
    return diagonal * field - 0.25 * (box_sum(padded) - field)


def squares(residual):
    return lax.psum(jnp.sum(residual * residual), ("gx", "gy"))


def local(fractions, normals, point_cells, block_owner, block_tile, block_count):
    devices = lax.axis_size(("gx", "gy"))
    blocks = fractions.shape[0]
    capacity = 2 * blocks // devices
    owner = block_owner[:, 0]
    targets = (owner[:, None] == jnp.arange(devices, dtype=jnp.int32)[None, :]).astype(jnp.int32)
    before = jnp.sum((jnp.cumsum(targets, axis=0) - targets) * targets, axis=1)
    slot_index = owner * capacity + before

    def arrange(rows):
        empty = jnp.zeros((devices * capacity,) + rows.shape[1:], rows.dtype)
        return empty.at[slot_index].set(rows).reshape((devices, capacity) + rows.shape[1:])

    header = jnp.stack([block_tile, block_count], axis=1)
    part_fractions = lax.all_to_all(
        arrange(fractions), ("gx", "gy"), split_axis=0, concat_axis=0, tiled=True
    )
    part_normals = lax.all_to_all(
        arrange(normals), ("gx", "gy"), split_axis=0, concat_axis=0, tiled=True
    )
    part_cells = lax.all_to_all(
        arrange(point_cells), ("gx", "gy"), split_axis=0, concat_axis=0, tiled=True
    )
    part_header = lax.all_to_all(
        arrange(header), ("gx", "gy"), split_axis=0, concat_axis=0, tiled=True
    )
    leading = part_fractions.shape[:2]
    made = splat_many(
        part_fractions.reshape((-1,) + part_fractions.shape[2:]),
        part_normals.reshape((-1,) + part_normals.shape[2:]),
        part_cells.reshape((-1,) + part_cells.shape[2:]),
        part_header[:, :, 1].reshape(-1),
    )
    tiles = made.reshape(leading + made.shape[1:])
    tile_ids = part_header[:, :, 0]
    fields = assemble(tiles, tile_ids)
    source = fields[0]
    diagonal = 6.5 + screen_weight * fields[1]
    solution_field = jnp.zeros_like(source)
    residual = source
    direction = source
    norm_now = squares(residual)
    for turn in range(ITERS):
        image = operate(direction, diagonal)
        alpha = norm_now / lax.psum(jnp.sum(direction * image), ("gx", "gy"))
        solution_field = solution_field + alpha * direction
        residual = residual - alpha * image
        norm_next = squares(residual)
        direction = residual + norm_next / norm_now * direction
        norm_now = norm_next
    return (solution_field, residual)


def solution(mesh):
    placed = (
        P(("gx", "gy"), None, None),
        P(("gx", "gy"), None, None),
        P(("gx", "gy"), None),
        P(("gx", "gy"), None),
        P(("gx", "gy")),
        P(("gx", "gy")),
    )
    return jax.shard_map(
        local,
        mesh=mesh,
        in_specs=placed,
        out_specs=(P(None, "gx", "gy"), P(None, "gx", "gy")),
        check_vma=False,
    )
```

profile of v0, /device:TPU:1, one launch (start us, length us, event | category | flops | bytes accessed | tf_op | source)
XLA Modules:
  0.0 774.6 jit_solution(4245964795324288400)
XLA Ops:
  6.3 11.5 %all-to-all-start = ((s32[128,2,2]{1,2,0:T(2,128)}), s32[128,2,2]{1,2,0:T(2,128)S(1)}, u32[]{:S(2)}, u32[]{:S(2)}) async-start(s32[128,2,2]{1,2,0:T(2,128)} %copy.48), calls=%async_computation | async-start | bytes 262144 | tf_op jit(solution)/shard_map/all_to_all | solution.py:127
  19.0 4.3 scatter_fusion
  24.2 3.5 all-to-all-done
  27.8 6.2 all-to-all-start.1
  34.2 4.3 scatter_fusion.1
  39.5 6.8 all-to-all-done.1
  46.3 4.6 all-to-all-start.3
  50.9 1.8 scatter_custom_fusion.2
  52.7 10.5 %all-to-all-done.3 = f32[128,2,3,128]{3,1,2,0:T(2,128)S(1)} async-done(((f32[128,2,3,128]{3,1,2,0:T(2,128)}), f32[128,2,3,128]{3,1,2,0:T(2,128)S(1)}, u32[]{:S(2)}, u32[]{:S(2)}) %all-to-all-start.3) | async-done | bytes 393248 | tf_op jit(solution)/shard_map/all_to_all | solution.py:118
  63.2 4.6 all-to-all-start.2
  69.3 8.5 %all-to-all-done.2 = s32[128,2,128]{2,1,0:T(2,128)S(1)} async-done(((s32[128,2,128]{2,1,0:T(2,128)}), s32[128,2,128]{2,1,0:T(2,128)S(1)}, u32[]{:S(2)}, u32[]{:S(2)}) %all-to-all-start.2) | async-done | bytes 131104 | tf_op jit(solution)/shard_map/all_to_all | solution.py:124
  77.8 205.2 %while.13 = (s32[]{:T(128)}, f32[2,128,2,128,16]{3,4,2,1,0:T(8,128)}, s32[2,128]{1,0:T(2,128)S(1)}, f32[2,128,3,128]{3,1,0,2:T(8,128)S(1)}, s32[2,128,128]{2,1,0...) while((s32[]{:T(128)}, f32[2,128,2,128,16]{3,4,2,1,0:T(8,128)}, s32[2,128]{1,0:T(2,128)S(1)}, ...), condition=%wide.region_7.8_spmd, body=%wide.region_6.7_spmd.sunk | while | flops 1649213440 | bytes 201460432 | solution.py:74
  94.7 8.9 %multiply_bitcast_fusion.5 = (f32[128,128,128]{1,2,0:T(8,128)}, f32[128,128,128]{1,2,0:T(8,128)}, f32[128,128,128]{1,2,0:T(8,128)}) fusion(f32[128,128,8]{1,2,0:T(8,128)S(1)} %get-tuple-element.276, f32[128,128,16]{1,2,0:T(8,128)S(1)} %get-tuple-element.269, f32[128,128,8]{1,2,0:T(8,128)S(1)} %get-tuple-element.264, ...), kind=kLoop, calls=%fused_computation.15.clone.1 | loop fusion | flops 6291456 | bytes 28311552 | tf_op jit(solution)/shard_map/while/body/eval_jaxpr/vmap()/mul | solution.py:49
  103.6 9.0 %copy.96 = f32[128,128,128]{2,1,0:T(8,128)} copy(f32[128,128,128]{1,2,0:T(8,128)} %get-tuple-element.281) | data formatting | bytes 16777216 | tf_op jit(solution)/shard_map/while/body/eval_jaxpr/vmap()/mul | solution.py:49
  112.7 7.9 %broadcast_multiply_fusion.7 = f32[128,128,128]{2,1,0:T(8,128)} fusion(f32[128,128,128]{2,1,0:T(8,128)} %copy.96, f32[128,128]{1,0:T(8,128)S(1)} %get-tuple-element.282), kind=kLoop, calls=%fused_computation.18.clone.1 | loop fusion | flops 2097152 | bytes 16842752 | tf_op jit(solution)/shard_map/while/body/eval_jaxpr/vmap()/mul | solution.py:55
  120.6 9.0 %copy.97 = f32[128,128,128]{2,1,0:T(8,128)} copy(f32[128,128,128]{1,2,0:T(8,128)} %get-tuple-element.283) | data formatting | bytes 16777216 | tf_op jit(solution)/shard_map/while/body/eval_jaxpr/vmap()/mul | solution.py:49
  129.6 7.9 %broadcast_multiply_fusion.8 = f32[128,128,128]{2,1,0:T(8,128)} fusion(f32[128,128,128]{2,1,0:T(8,128)} %copy.97, f32[128,128]{1,0:T(8,128)S(1)} %get-tuple-element.284), kind=kLoop, calls=%fused_computation.19.clone.1 | loop fusion | flops 2097152 | bytes 16842752 | tf_op jit(solution)/shard_map/while/body/eval_jaxpr/vmap()/mul | solution.py:54
  137.5 9.0 %copy.95 = f32[128,128,128]{2,1,0:T(8,128)} copy(f32[128,128,128]{1,2,0:T(8,128)} %get-tuple-element.278) | data formatting | bytes 16777216 | tf_op jit(solution)/shard_map/while/body/eval_jaxpr/vmap()/mul | solution.py:49
  146.5 8.0 %broadcast_multiply_fusion.6 = f32[128,128,128]{2,1,0:T(8,128)S(1)} fusion(f32[128,128,128]{2,1,0:T(8,128)} %copy.95, f32[128,128]{1,0:T(8,128)S(1)} %get-tuple-element.280), kind=kLoop, calls=%fused_computation.17.clone.1 | loop fusion | flops 2097152 | bytes 16842752 | tf_op jit(solution)/shard_map/while/body/eval_jaxpr/vmap()/mul | solution.py:56
  154.9 18.3 %fusion.79 = f32[1,128,128,16]{2,3,1,0:T(8,128)S(1)} fusion(f32[128,128,16]{1,2,0:T(8,128)S(1)} %get-tuple-element.274, f32[128,128,16]{1,2,0:T(8,128)S(1)} %get-tuple-element.275, f32[128,128,128]{2,1,0:T(8,128)S(1)} %broadcast_multiply_fusion.6, f32[128,128,128]{2,1,0:T(8,128)S(1)} %bitcast.140, f32[128,128,128]{2,1,0:T(8,128)} %broadcast_multiply_fusion.8), kind=kOutput, calls=%fused_computation.28.clone.1 | convolution fusion | flops 1222115328 | bytes 28311552 | tf_op jit(solution)/shard_map/while/body/eval_jaxpr/vmap()/dot_general | solution.py:61
  173.2 13.4 %fusion.77 = f32[1,128,128,16]{2,3,1,0:T(8,128)S(1)} fusion(f32[128,128]{1,0:T(8,128)S(1)} %fusion.76, f32[128,128,8]{1,2,0:T(8,128)S(1)} %get-tuple-element.264, f32[128,128,16]{1,2,0:T(8,128)S(1)} %get-tuple-element.269, f32[128,128]{1,0:T(8,128)S(1)} %get-tuple-element.270, s32[128,128]{1,0:T(8,128)S(1)} %get-tuple-element.271, ...), kind=kOutput, calls=%fused_computation.27.clone.1 | convolution fusion | flops 408158208 | bytes 2949120 | tf_op jit(solution)/shard_map/while/body/eval_jaxpr/vmap()/dot_general | solution.py:64
  189.5 8.9 %multiply_bitcast_fusion.5 = (f32[128,128,128]{1,2,0:T(8,128)}, f32[128,128,128]{1,2,0:T(8,128)}, f32[128,128,128]{1,2,0:T(8,128)}) fusion(f32[128,128,8]{1,2,0:T(8,128)S(1)} %get-tuple-element.276, f32[128,128,16]{1,2,0:T(8,128)S(1)} %get-tuple-element.269, f32[128,128,8]{1,2,0:T(8,128)S(1)} %get-tuple-element.264, ...), kind=kLoop, calls=%fused_computation.15.clone.1 | loop fusion | flops 6291456 | bytes 28311552 | tf_op jit(solution)/shard_map/while/body/eval_jaxpr/vmap()/mul | solution.py:49
  198.5 9.0 %copy.96 = f32[128,128,128]{2,1,0:T(8,128)} copy(f32[128,128,128]{1,2,0:T(8,128)} %get-tuple-element.281) | data formatting | bytes 16777216 | tf_op jit(solution)/shard_map/while/body/eval_jaxpr/vmap()/mul | solution.py:49
  207.6 7.9 %broadcast_multiply_fusion.7 = f32[128,128,128]{2,1,0:T(8,128)} fusion(f32[128,128,128]{2,1,0:T(8,128)} %copy.96, f32[128,128]{1,0:T(8,128)S(1)} %get-tuple-element.282), kind=kLoop, calls=%fused_computation.18.clone.1 | loop fusion | flops 2097152 | bytes 16842752 | tf_op jit(solution)/shard_map/while/body/eval_jaxpr/vmap()/mul | solution.py:55
  215.5 9.0 %copy.97 = f32[128,128,128]{2,1,0:T(8,128)} copy(f32[128,128,128]{1,2,0:T(8,128)} %get-tuple-element.283) | data formatting | bytes 16777216 | tf_op jit(solution)/shard_map/while/body/eval_jaxpr/vmap()/mul | solution.py:49
  224.5 7.9 %broadcast_multiply_fusion.8 = f32[128,128,128]{2,1,0:T(8,128)} fusion(f32[128,128,128]{2,1,0:T(8,128)} %copy.97, f32[128,128]{1,0:T(8,128)S(1)} %get-tuple-element.284), kind=kLoop, calls=%fused_computation.19.clone.1 | loop fusion | flops 2097152 | bytes 16842752 | tf_op jit(solution)/shard_map/while/body/eval_jaxpr/vmap()/mul | solution.py:54
  232.4 9.0 %copy.95 = f32[128,128,128]{2,1,0:T(8,128)} copy(f32[128,128,128]{1,2,0:T(8,128)} %get-tuple-element.278) | data formatting | bytes 16777216 | tf_op jit(solution)/shard_map/while/body/eval_jaxpr/vmap()/mul | solution.py:49
  241.4 8.0 %broadcast_multiply_fusion.6 = f32[128,128,128]{2,1,0:T(8,128)S(1)} fusion(f32[128,128,128]{2,1,0:T(8,128)} %copy.95, f32[128,128]{1,0:T(8,128)S(1)} %get-tuple-element.280), kind=kLoop, calls=%fused_computation.17.clone.1 | loop fusion | flops 2097152 | bytes 16842752 | tf_op jit(solution)/shard_map/while/body/eval_jaxpr/vmap()/mul | solution.py:56
  249.7 18.3 %fusion.79 = f32[1,128,128,16]{2,3,1,0:T(8,128)S(1)} fusion(f32[128,128,16]{1,2,0:T(8,128)S(1)} %get-tuple-element.274, f32[128,128,16]{1,2,0:T(8,128)S(1)} %get-tuple-element.275, f32[128,128,128]{2,1,0:T(8,128)S(1)} %broadcast_multiply_fusion.6, f32[128,128,128]{2,1,0:T(8,128)S(1)} %bitcast.140, f32[128,128,128]{2,1,0:T(8,128)} %broadcast_multiply_fusion.8), kind=kOutput, calls=%fused_computation.28.clone.1 | convolution fusion | flops 1222115328 | bytes 28311552 | tf_op jit(solution)/shard_map/while/body/eval_jaxpr/vmap()/dot_general | solution.py:61
  268.1 13.4 %fusion.77 = f32[1,128,128,16]{2,3,1,0:T(8,128)S(1)} fusion(f32[128,128]{1,0:T(8,128)S(1)} %fusion.76, f32[128,128,8]{1,2,0:T(8,128)S(1)} %get-tuple-element.264, f32[128,128,16]{1,2,0:T(8,128)S(1)} %get-tuple-element.269, f32[128,128]{1,0:T(8,128)S(1)} %get-tuple-element.270, s32[128,128]{1,0:T(8,128)S(1)} %get-tuple-element.271, ...), kind=kOutput, calls=%fused_computation.27.clone.1 | convolution fusion | flops 408158208 | bytes 2949120 | tf_op jit(solution)/shard_map/while/body/eval_jaxpr/vmap()/dot_general | solution.py:64
  283.7 22.7 %scatter_fusion.2 = f32[128,2,128,16]{2,3,1,0:T(8,128)S(1)} fusion(f32[128,2,128,16]{2,3,1,0:T(8,128)S(1)} %broadcast_in_dim.15, s32[256]{0:T(256)S(1)} %copy-done.6, f32[256,2,128,16]{2,3,1,0:T(8,128)} %bitcast.31), kind=kCustom, calls=%fused_computation.4 | custom fusion | flops 1048576 | bytes 12583936 | tf_op jit(solution)/shard_map/scatter-add | solution.py:83
  306.4 2.3 copy.58
  308.7 10.6 %reshape.370 = f32[8,16,2,16,8,16]{1,0,5,4,3,2:T(8,128)} reshape(f32[128,2,128,16]{0,3,2,1:T(8,128)} %copy.58) | data formatting | bytes 4194304 | tf_op jit(solution)/shard_map/reshape | solution.py:84
  319.3 11.8 %multiply_reduce_fusion = (f32[]{:T(128)}, f32[1,16,8,8,16,16]{4,2,5,3,1,0:T(8,128)}, f32[1,16,8,8,16,16]{4,2,5,3,1,0:T(8,128)}) fusion(f32[2,16,8,8,16,16]{4,2,5,3,1,0:T(8,128)} %bitcast.141), kind=kLoop, calls=%fused_computation.79 | loop fusion | flops 1048575 | bytes 4194308 | tf_op jit(solution)/shard_map/reduce_sum | solution.py:101
  331.1 9.3 %copy.59 = f32[1,16,8,8,16,16]{5,4,3,2,1,0:T(8,128)} copy(f32[1,16,8,8,16,16]{4,2,5,3,1,0:T(8,128)} %get-tuple-element.181) | data formatting | bytes 2097152 | tf_op jit(solution)/shard_map/slice | solution.py:140
  340.4 6.1 squeeze.45
  346.5 2.0 collective-permute-start
  349.8 3.2 collective-permute-done.1
  353.6 4.2 collective-permute-start.2
  358.0 1.9 collective-permute-start.3
  360.0 9.3 %copy.60 = f32[1,16,8,8,16,16]{5,4,3,2,1,0:T(8,128)} copy(f32[1,16,8,8,16,16]{4,2,5,3,1,0:T(8,128)} %get-tuple-element.180) | data formatting | bytes 2097152 | tf_op jit(solution)/shard_map/add | solution.py:141
  369.3 6.1 add.262
  376.8 1.9 pad_maximum_fusion
  380.5 66.2 %all-reduce.3 = (f32[]{:T(128)}, f32[]{:T(128)}) all-reduce(f32[]{:T(128)} %get-tuple-element.179, f32[]{:T(128)} %get-tuple-element.153), channel_id=1, replica_groups=mesh['gx'=16,'gy'=8] {'gx','gy'}, use_global_device_ids=true, to_apply=%region_10.11 | all-reduce | flops 2 | bytes 16 | tf_op jit(solution)/shard_map/psum | solution.py:101
  448.9 63.2 %psum.44 = f32[]{:T(128)} all-reduce(f32[]{:T(128)} %multiply_reduce_fusion.4), channel_id=1, replica_groups=mesh['gx'=16,'gy'=8] {'gx','gy'}, use_global_device_ids=true, to_apply=%region_14.15 | all-reduce | flops 1 | bytes 8 | tf_op jit(solution)/shard_map/psum | solution.py:101
  514.9 2.3 collective-permute-start.4
  518.5 3.2 collective-permute-done.5
  524.3 3.7 collective-permute-start.6
  529.3 1.9 collective-permute-start.7
  532.4 1.9 collective-permute-done.7
  535.4 2.1 pad_maximum_fusion.1
  538.0 2.3 multiply_reduce_fusion.3
  540.3 66.1 %psum.45 = f32[]{:T(128)} all-reduce(f32[]{:T(128)} %get-tuple-element.151), channel_id=1, replica_groups=mesh['gx'=16,'gy'=8] {'gx','gy'}, use_global_device_ids=true, to_apply=%region_16.17 | all-reduce | flops 1 | bytes 8 | tf_op jit(solution)/shard_map/psum | solution.py:148
  607.7 3.4 multiply_reduce_fusion.2
  611.1 63.3 %psum.46 = f32[]{:T(128)} all-reduce(f32[]{:T(128)} %get-tuple-element.149), channel_id=1, replica_groups=mesh['gx'=16,'gy'=8] {'gx','gy'}, use_global_device_ids=true, to_apply=%region_18.19 | all-reduce | flops 1 | bytes 8 | tf_op jit(solution)/shard_map/psum | solution.py:101
  677.2 1.8 collective-permute-start.8
  680.3 3.2 collective-permute-done.9
  686.1 4.5 collective-permute-start.10
  691.8 1.9 collective-permute-start.11
  694.9 1.9 collective-permute-done.11
  697.9 2.1 pad_maximum_fusion.2
  701.4 2.2 multiply_reduce_fusion.1
  703.6 66.1 %psum.47 = f32[]{:T(128)} all-reduce(f32[]{:T(128)} %get-tuple-element.147), channel_id=1, replica_groups=mesh['gx'=16,'gy'=8] {'gx','gy'}, use_global_device_ids=true, to_apply=%region_20.21 | all-reduce | flops 1 | bytes 8 | tf_op jit(solution)/shard_map/psum | solution.py:148
  771.0 3.3 multiply_subtract_fusion
  (112 shorter events, 43.8 us)
Async XLA Ops:
  6.3 21.5 %all-to-all-start = ((s32[128,2,2]{1,2,0:T(2,128)}), s32[128,2,2]{1,2,0:T(2,128)S(1)}, u32[]{:S(2)}, u32[]{:S(2)}) async-start(s32[128,2,2]{1,2,0:T(2,128)} %copy.48), calls=%async_computation | async-start | bytes 262144 | tf_op jit(solution)/shard_map/all_to_all | solution.py:127
  17.8 16.3 %copy-start.5 = (f32[128,3,128]{2,0,1:T(8,128)S(1)}, f32[128,3,128]{2,0,1:T(8,128)}, u32[]{:S(2)}) copy-start(f32[128,3,128]{2,0,1:T(8,128)} %param.8) | copy-start | bytes 589828
  27.8 18.5 %all-to-all-start.1 = ((f32[128,2,3,128]{3,1,2,0:T(2,128)}), f32[128,2,3,128]{3,1,2,0:T(2,128)S(1)}, u32[]{:S(2)}, u32[]{:S(2)}) async-start(f32[128,2,3,128]{3,1,2,0:T(2,128)} %copy.50), calls=%async_computation.1 | async-start | bytes 786432 | tf_op jit(solution)/shard_map/all_to_all | solution.py:121
  46.3 16.9 %all-to-all-start.3 = ((f32[128,2,3,128]{3,1,2,0:T(2,128)}), f32[128,2,3,128]{3,1,2,0:T(2,128)S(1)}, u32[]{:S(2)}, u32[]{:S(2)}) async-start(f32[128,2,3,128]{3,1,2,0:T(2,128)} %copy.53), calls=%async_computation.3 | async-start | bytes 786432 | tf_op jit(solution)/shard_map/all_to_all | solution.py:118
  63.2 14.6 %all-to-all-start.2 = ((s32[128,2,128]{2,1,0:T(2,128)}), s32[128,2,128]{2,1,0:T(2,128)S(1)}, u32[]{:S(2)}, u32[]{:S(2)}) async-start(s32[128,2,128]{2,1,0:T(2,128)} %bitcast.27), calls=%async_computation.2 | async-start | bytes 262144 | tf_op jit(solution)/shard_map/all_to_all | solution.py:124
  93.2 0.7 copy-start.3
  146.5 8.4 %slice-start = ((s8[8388608]{0:T(1024)(128)(4,1)}), s8[4194304]{0:T(1024)(128)(4,1)S(1)}, s32[]{:S(2)}) async-start(s8[8388608]{0:T(1024)(128)(4,1)} %bitcast.139), calls=%async_computation.4 | async-start | bytes 8388608 | tf_op jit(solution)/shard_map/while
  146.5 8.4 %slice-start.1 = ((s8[8388608]{0:T(1024)(128)(4,1)}), s8[4194304]{0:T(1024)(128)(4,1)S(1)}, s32[]{:S(2)}) async-start(s8[8388608]{0:T(1024)(128)(4,1)} %bitcast.139), calls=%async_computation.5 | async-start | bytes 8388608 | tf_op jit(solution)/shard_map/while
  186.6 1.5 copy-start.4
  188.1 0.7 copy-start.3
  241.4 8.4 %slice-start = ((s8[8388608]{0:T(1024)(128)(4,1)}), s8[4194304]{0:T(1024)(128)(4,1)S(1)}, s32[]{:S(2)}) async-start(s8[8388608]{0:T(1024)(128)(4,1)} %bitcast.139), calls=%async_computation.4 | async-start | bytes 8388608 | tf_op jit(solution)/shard_map/while
  241.4 8.4 %slice-start.1 = ((s8[8388608]{0:T(1024)(128)(4,1)}), s8[4194304]{0:T(1024)(128)(4,1)S(1)}, s32[]{:S(2)}) async-start(s8[8388608]{0:T(1024)(128)(4,1)} %bitcast.139), calls=%async_computation.5 | async-start | bytes 8388608 | tf_op jit(solution)/shard_map/while
  281.5 1.5 copy-start.4
  283.0 0.7 copy-start.6
  346.5 3.3 collective-permute-start
  348.5 4.5 collective-permute-start.1
  353.6 21.8 %collective-permute-start.2 = (f32[16,66,1]{1,0,2:T(8,128)S(1)}, f32[16,66,1]{1,0,2:T(8,128)S(1)}, u32[]{:S(2)}, u32[]{:S(2)}) collective-permute-start(f32[16,66,1]{1,0,2:T(8,128)S(1)} %copy.61), channel_id=1, source_target_pairs={{0,1},{1,2},{2,3},{3,4},{4,5},{5,6},{6,7},{8,9},{9,10},{10,11},{11... | collective-permute-start | bytes 12680 | tf_op jit(solution)/shard_map/ppermute | solution.py:22
  358.0 17.7 %collective-permute-start.3 = (f32[16,66,1]{1,0,2:T(8,128)S(1)}, f32[16,66,1]{1,0,2:T(8,128)S(1)}, u32[]{:S(2)}, u32[]{:S(2)}) collective-permute-start(f32[16,66,1]{1,0,2:T(8,128)S(1)} %copy.62), channel_id=1, source_target_pairs={{1,0},{2,1},{3,2},{4,3},{5,4},{6,5},{7,6},{9,8},{10,9},{11,10},{12... | collective-permute-start | bytes 12680 | tf_op jit(solution)/shard_map/ppermute | solution.py:25
  375.4 162.6 %copy-start = (f32[16,64,256]{2,1,0:T(8,128)}, f32[16,64,256]{2,1,0:T(8,128)S(1)}, u32[]{:S(2)}) copy-start(f32[16,64,256]{2,1,0:T(8,128)S(1)} %add.262) | copy-start | bytes 3145732
  380.5 131.6 %copy-start.2 = (f32[16,64,256]{2,1,0:T(8,128)}, f32[16,64,256]{2,1,0:T(8,128)S(1)}, u32[]{:S(2)}) copy-start(f32[16,64,256]{2,1,0:T(8,128)S(1)} %get-tuple-element.154) | copy-start | bytes 3145732
  514.9 3.6 collective-permute-start.4
  517.2 4.5 collective-permute-start.5
  524.3 7.0 collective-permute-start.6
  529.3 5.0 collective-permute-start.7
  677.2 3.1 collective-permute-start.8
  679.0 4.5 collective-permute-start.9
  686.1 7.7 collective-permute-start.10
  691.8 5.0 collective-permute-start.11
  700.2 1.2 copy-start.1
where the time goes:
time: 783 us; the launch traced here: 775 us
  blocking collectives  325 us (42%)
  other arithmetic  133 us (17%)
  local copies, waits for them, and re-layouts  133 us (17%)
  matrix products  63.3 us (8%)
  starting transfers between devices  55 us (7%)
  waiting for transfers between devices  42.7 us (5%)
  loops' own time  15.6 us (2%)
    psum x3, blocking collectives, squares(): return lax.psum(jnp.sum(residual * residual), ('gx', 'gy'))  193 us
    psum x2, blocking collectives, local(): alpha = norm_now / lax.psum(jnp.sum(direction * image), ('gx', 'gy'))  132 us
    mul x6, local copies, waits for them, and re-layouts, outer_pair(): return (first[:, :, None] * second[:, None, :]).reshape(points, CZ * TX)  54 us
    dot_general x2, matrix products, splat_block(): jnp.dot(left.T, right, precision=lax.Precision.HIGHEST, preferred_element...  36.5 us
    dot_general x2, matrix products, splat_block(): jnp.dot((valid[:, None] * shared).T, weight_y, precision=lax.Precision.HI...  26.7 us
    scatter-add x1, other arithmetic, assemble(): jax.ops.segment_sum(flat, tile_ids.reshape(-1), num_segments=tiles_x * ti...  22.7 us
    ppermute x6, starting transfers between devices, with_halo(): lax.ppermute(lax.slice_in_dim(block, block.shape[dim] - width, None, axis...  18.5 us
    mul x2, other arithmetic, outer_pair(): return (first[:, :, None] * second[:, None, :]).reshape(points, CZ * TX)  17.9 us
  transfers between devices with their start and end apart: 16, of which 9 were waited for; matrix products, arithmetic and copies ran while one was open for 5% of the time, Pallas kernels for 0%

commit v1 on v0

v1 whole, which is shorter than its diff:
```python
import jax
import jax.numpy as jnp
from jax import lax
from jax.experimental import pallas as pl
from jax.experimental.pallas import tpu as pltpu
from jax.sharding import PartitionSpec as P

CX = 64
CY = 256
CZ = 16
TX = 8
TY = 16
POINTS = 128
ITERS = 3
LANES = 128
GROUP = 4

screen_weight = 4.0
MESH = pl.DeviceIdType.MESH


def arrange_kernel(slot_ref, tile_ref, count_ref, frac_ref, norm_ref, cell_ref, out_ref):
    blocks = frac_ref.shape[0]
    lane = lax.broadcasted_iota(jnp.int32, (1, LANES), 1)
    out_ref[...] = jnp.zeros_like(out_ref)

    def place(k, carry):
        slot = slot_ref[k]
        out_ref[slot, 0:3, :] = frac_ref[k]
        out_ref[slot, 3:6, :] = norm_ref[k]
        out_ref[slot, 6:7, :] = cell_ref[pl.ds(k, 1), :].astype(jnp.float32)
        header = jnp.where(lane == 0, tile_ref[k], jnp.where(lane == 1, count_ref[k], 0))
        out_ref[slot, 7:8, :] = header.astype(jnp.float32)
        return carry

    lax.fori_loop(0, blocks, place, 0)


def arrange(slot, tile, count, fractions, normals, cells, slots):
    smem = pl.BlockSpec(memory_space=pltpu.SMEM)
    vmem = pl.BlockSpec(memory_space=pltpu.VMEM)
    return pl.pallas_call(
        arrange_kernel,
        out_shape=jax.ShapeDtypeStruct((slots, 8, LANES), jnp.float32),
        in_specs=[smem, smem, smem, vmem, vmem, vmem],
        out_specs=vmem,
        compiler_params=pltpu.CompilerParams(vmem_limit_bytes=16 << 20),
    )(slot, tile, count, fractions, normals, cells)


def split(value):
    high = value.astype(jnp.bfloat16)
    return high, (value - high.astype(jnp.float32)).astype(jnp.bfloat16)


def taps(anchor, offset, length):
    place = lax.broadcasted_iota(jnp.int32, (length, POINTS), 0).astype(jnp.float32)
    lower = place == anchor
    upper = place == anchor + 1.0
    weight = jnp.where(lower, 1.0 - offset, jnp.where(upper, offset, 0.0))
    slope = jnp.where(lower, -1.0, jnp.where(upper, 1.0, 0.0))
    return weight, slope


def splat_tile(block, count):
    lane = lax.broadcasted_iota(jnp.int32, (1, POINTS), 1)
    valid = lane < count
    cell = block[6:7]
    remains = jnp.floor((cell + 0.5) * (1.0 / (CZ - 1)))
    plane = cell - remains * (CZ - 1)
    row = jnp.floor((remains + 0.5) * (1.0 / (TY - 1)))
    column = remains - row * (TY - 1)
    row = jnp.where(valid, row, -4.0)
    wx, sx = taps(row, block[0:1], TX)
    wy, sy = taps(column, block[1:2], TY)
    wz, sz = taps(plane, block[2:3], CZ)
    sx = sx * block[3:4]
    sy = sy * block[4:5]
    tx = wx * block[5:6]
    first = jnp.concatenate(
        [wz[z : z + 1] * sx + sz[z : z + 1] * tx for z in range(CZ)], axis=0
    )
    second = jnp.concatenate([wz[z : z + 1] * wx for z in range(CZ)], axis=0)
    big = jnp.concatenate([first, second], axis=1)
    top = jnp.concatenate([wy, sy], axis=1)
    low = jnp.concatenate([jnp.zeros_like(wy), wy], axis=1)
    small = jnp.concatenate([top, low], axis=0)
    big_high, big_low = split(big)
    small_high, small_low = split(small)
    dims = (((1,), (1,)), ((), ()))
    both = lax.dot_general(
        jnp.concatenate([small_high, small_low], axis=0),
        big_high,
        dims,
        preferred_element_type=jnp.float32,
    )
    rest = lax.dot_general(small_high, big_low, dims, preferred_element_type=jnp.float32)
    return both[: 2 * TY] + both[2 * TY :] + rest


def splat_kernel(tile_ref, count_ref, blocks_ref, acc_ref, order):
    slots = blocks_ref.shape[0]
    acc_ref[...] = jnp.zeros_like(acc_ref)

    def gather(i, carry):
        used, empty = carry
        some = count_ref[i] > 0

        @pl.when(some)
        def _():
            order[used] = i

        return used + some.astype(jnp.int32), jnp.where(some, empty, i)

    used, empty = lax.fori_loop(0, slots, gather, (jnp.int32(0), jnp.int32(0)))
    for extra in range(GROUP):
        order[used + extra] = empty

    def work(j, carry):
        made = []
        for u in range(GROUP):
            slot = order[j * GROUP + u]
            made.append((tile_ref[slot], splat_tile(blocks_ref[slot], count_ref[slot])))
        tiles_y = CY // TY
        for tile, values in made:
            x = tile // tiles_y
            y = pl.multiple_of((tile % tiles_y) * TY, TY)
            acc_ref[x, 0, pl.ds(y, TY), :] += values[:TY]
            acc_ref[x, 1, pl.ds(y, TY), :] += values[TY:]
        return carry

    lax.fori_loop(0, (used + GROUP - 1) // GROUP, work, 0)


def splat(tile, count, blocks):
    slots = blocks.shape[0]
    smem = pl.BlockSpec(memory_space=pltpu.SMEM)
    vmem = pl.BlockSpec(memory_space=pltpu.VMEM)
    return pl.pallas_call(
        splat_kernel,
        out_shape=jax.ShapeDtypeStruct((CX // TX, 2, CY, CZ * TX), jnp.float32),
        in_specs=[smem, smem, vmem],
        out_specs=vmem,
        scratch_shapes=[pltpu.SMEM((slots + GROUP,), jnp.int32)],
        compiler_params=pltpu.CompilerParams(vmem_limit_bytes=24 << 20),
    )(tile, count, blocks)


def fold(value):
    total = value[0:8]
    for k in range(1, value.shape[0] // 8):
        total = total + value[8 * k : 8 * k + 8]
    return total


def solve_kernel(
    count_x, count_y,
    acc_ref, x_ref, r_ref,
    rp, dg, p, s, w, rim,
    row_out, row_in, col_out, col_in, part_y, part_x, got_y, got_x,
    row_s, row_r, col_s, col_r, y_s, y_r, x_s, x_r,
):
    me_x, me_y = lax.axis_index("gx"), lax.axis_index("gy")

    def at(dx, dy):
        return (lax.rem(me_x + dx + count_x, count_x), lax.rem(me_y + dy + count_y, count_y))

    barrier = pltpu.get_barrier_semaphore()

    def greet_y(d, carry):
        pl.semaphore_signal(barrier, inc=1, device_id=at(0, d), device_id_type=MESH)
        return carry

    def greet_x(d, carry):
        pl.semaphore_signal(barrier, inc=1, device_id=at(d, 0), device_id_type=MESH)
        return carry

    lax.fori_loop(1, count_y, greet_y, 0)
    lax.fori_loop(1, count_x, greet_x, 0)
    for dx in (-1, 1):
        for dy in (-1, 1):
            pl.semaphore_signal(barrier, inc=1, device_id=at(dx, dy), device_id_type=MESH)

    sub8 = lax.broadcasted_iota(jnp.int32, (8, LANES), 0)
    lane8 = lax.broadcasted_iota(jnp.int32, (8, LANES), 1)
    lane_half = lax.broadcasted_iota(jnp.int32, (CX, LANES), 1)
    row_half = lax.broadcasted_iota(jnp.int32, (CX, LANES), 0)

    rp[0] = jnp.zeros((CX, CY), jnp.float32)
    rp[CZ + 1] = jnp.zeros((CX, CY), jnp.float32)

    def unfold(t, carry):
        rows = pl.ds(pl.multiple_of(t * TX, TX), TX)
        source = acc_ref[t, 0].T.reshape(CZ, TX, CY)
        density = acc_ref[t, 1].T.reshape(CZ, TX, CY)
        rp[1 : CZ + 1, rows, :] = source
        dg[:, rows, :] = 6.75 + screen_weight * density
        return carry

    lax.fori_loop(0, CX // TX, unfold, 0)

    def clear(z, carry):
        zero = jnp.zeros((CX, CY), jnp.float32)
        p[z] = zero
        s[z] = zero
        x_ref[z] = zero
        return carry

    lax.fori_loop(0, CZ, clear, 0)
    pl.semaphore_wait(barrier, (count_y - 1) + (count_x - 1) + 4)

    def pack(z, carry):
        west, east = carry
        for t in range(CX // TX):
            here = rp[z + 1, 8 * t : 8 * t + 8, :]
            shift = z + CZ * t
            mine = lane8 == shift
            west = jnp.where(mine, pltpu.roll(here[:, :LANES], shift, 1), west)
            turned = pltpu.roll(here[:, LANES:], lax.rem(shift + 1, LANES), 1)
            east = jnp.where(mine, turned, east)
        return west, east

    def ask(count, target, src, dst, send, recv):
        pltpu.make_async_remote_copy(
            src_ref=src, dst_ref=dst, send_sem=send, recv_sem=recv,
            device_id=target, device_id_type=MESH,
        ).start()

    def wait_for(ref, sem):
        pltpu.make_async_copy(ref, ref, sem).wait()

    zero8 = jnp.zeros((8, LANES), jnp.float32)

    def total_of(parts):
        total = parts[0]
        for k in range(1, parts.shape[0]):
            total = total + parts[k]
        return total

    def turn(it, carry):
        gamma_old, curve_old = carry
        row_out[it, 0] = rp[1 : CZ + 1, 0, :]
        row_out[it, 1] = rp[1 : CZ + 1, CX - 1, :]
        ask(0, at(-1, 0), row_out.at[it, 0], row_in.at[it, 1], row_s.at[it], row_r.at[it])
        ask(0, at(1, 0), row_out.at[it, 1], row_in.at[it, 0], row_s.at[it], row_r.at[it])
        west, east = lax.fori_loop(0, CZ, pack, (zero8, zero8))
        col_out[it, 0] = west
        col_out[it, 1] = east
        for dx in (-1, 0, 1):
            ask(0, at(dx, -1), col_out.at[it, 0], col_in.at[it, 1, 1 - dx], col_s.at[it], col_r.at[it])
            ask(0, at(dx, 1), col_out.at[it, 1], col_in.at[it, 0, 1 - dx], col_s.at[it], col_r.at[it])

        wait_for(row_in.at[it], row_r.at[it])
        zrow = lax.broadcasted_iota(jnp.int32, (CZ, CY), 0)
        for side, there in ((0, me_x > 0), (1, me_x < count_x - 1)):
            near = row_in[it, side]
            near = (
                near
                + jnp.where(zrow > 0, pltpu.roll(near, 1, 0), 0.0)
                + jnp.where(zrow < CZ - 1, pltpu.roll(near, CZ - 1, 0), 0.0)
            )
            near = jnp.where(there, near, 0.0)
            rim[side, 0] = near[:, :LANES]
            rim[side, 1] = near[:, LANES:]
        wait_for(col_in.at[it], col_r.at[it])

        plane8 = lax.rem(lane8, CZ)

        def column(side, there):
            def summed(k, ok):
                col = col_in[it, side, k]
                col = (
                    col
                    + jnp.where(plane8 > 0, pltpu.roll(col, 1, 1), 0.0)
                    + jnp.where(plane8 < CZ - 1, pltpu.roll(col, LANES - 1, 1), 0.0)
                )
                return jnp.where(ok, col, 0.0)

            mid = summed(1, there)
            low = summed(0, jnp.logical_and(there, me_x > 0))
            high = summed(2, jnp.logical_and(there, me_x < count_x - 1))

            def down(v):
                return pltpu.roll(v, 1, 0)

            def up(v):
                return pltpu.roll(v, 7, 0)

            before = jnp.where(lane8 < CZ, pltpu.roll(down(low), CZ, 1), pltpu.roll(down(mid), CZ, 1))
            before = jnp.where(sub8 == 0, before, down(mid))
            after = jnp.where(
                lane8 >= LANES - CZ,
                pltpu.roll(up(high), LANES - CZ, 1),
                pltpu.roll(up(mid), LANES - CZ, 1),
            )
            after = jnp.where(sub8 == 7, after, up(mid))
            return before + mid + after

        west_in = column(0, me_y > 0)
        east_in = column(1, me_y < count_y - 1)

        def apply(z, sums):
            gamma, delta, eta = sums
            halves = []
            for h in range(2):
                cols = slice(h * LANES, (h + 1) * LANES)
                u = rp[z, :, cols] + rp[z + 1, :, cols] + rp[z + 2, :, cols]
                above = rim[0, h, pl.ds(z, 1), :]
                below = rim[1, h, pl.ds(z, 1), :]
                t = (
                    u
                    + jnp.where(row_half == 0, above, pltpu.roll(u, 1, 0))
                    + jnp.where(row_half == CX - 1, below, pltpu.roll(u, CX - 1, 0))
                )
                halves.append(t)
            left, right = halves
            back = lax.rem(2 * LANES - z, LANES)
            west_col = jnp.concatenate(
                [pltpu.roll(west_in, lax.rem(back + LANES - CZ * t, LANES), 1) for t in range(CX // TX)],
                axis=0,
            )
            east_col = jnp.concatenate(
                [pltpu.roll(east_in, lax.rem(back + 2 * LANES - 1 - CZ * t, LANES), 1) for t in range(CX // TX)],
                axis=0,
            )
            lr, rr = pltpu.roll(left, 1, 1), pltpu.roll(right, 1, 1)
            ll, rl = pltpu.roll(left, LANES - 1, 1), pltpu.roll(right, LANES - 1, 1)
            first, last = lane_half == 0, lane_half == LANES - 1
            box_left = left + jnp.where(first, west_col, lr) + jnp.where(last, rl, ll)
            box_right = right + jnp.where(first, lr, rr) + jnp.where(last, east_col, rl)
            for h, box in ((0, box_left), (1, box_right)):
                cols = slice(h * LANES, (h + 1) * LANES)
                v = rp[z + 1, :, cols]
                image = dg[z, :, cols] * v - 0.25 * box
                w[z, :, cols] = image
                gamma = gamma + fold(v * v)
                delta = delta + fold(v * image)
                eta = eta + fold(v * s[z, :, cols])
            return gamma, delta, eta

        gamma, delta, eta = lax.fori_loop(0, CZ, apply, (zero8, zero8, zero8))
        gamma = jnp.sum(gamma, axis=0, keepdims=True)
        delta = jnp.sum(delta, axis=0, keepdims=True)
        eta = jnp.sum(eta, axis=0, keepdims=True)
        mine = jnp.where(sub8 == 0, gamma, jnp.where(sub8 == 1, delta, jnp.where(sub8 == 2, eta, 0.0)))
        part_y[it] = mine
        got_y[it, me_y] = mine

        def send_y(d, c):
            ask(0, at(0, d), part_y.at[it], got_y.at[it, me_y], y_s.at[it], y_r.at[it])
            return c

        lax.fori_loop(1, count_y, send_y, 0)
        wait_for(got_y.at[it, pl.ds(0, count_y - 1)], y_r.at[it])
        mine = total_of(got_y.at[it])
        part_x[it] = mine
        got_x[it, me_x] = mine

        def send_x(d, c):
            ask(0, at(d, 0), part_x.at[it], got_x.at[it, me_x], x_s.at[it], x_r.at[it])
            return c

        lax.fori_loop(1, count_x, send_x, 0)
        wait_for(got_x.at[it, pl.ds(0, count_x - 1)], x_r.at[it])
        total = jnp.sum(total_of(got_x.at[it]), axis=1, keepdims=True)
        gamma, delta, eta = total[0:1], total[1:2], total[2:3]
        beta = jnp.where(it == 0, 0.0, gamma / gamma_old)
        curve = delta + 2.0 * beta * eta + beta * beta * curve_old
        alpha = gamma / curve

        def update(z, c):
            r = rp[z + 1]
            pn = r + beta * p[z]
            sn = w[z] + beta * s[z]
            p[z] = pn
            s[z] = sn
            x_ref[z] = x_ref[z] + alpha * pn
            r = r - alpha * sn
            rp[z + 1] = r
            r_ref[z] = r
            return c

        lax.fori_loop(0, CZ, update, 0)
        return gamma, curve

    one = jnp.ones((1, 1), jnp.float32)
    lax.fori_loop(0, ITERS, turn, (one, 0.0 * one))

    def finish(it, c):
        wait_for(row_out.at[it], row_s.at[it])
        wait_for(col_in.at[it], col_s.at[it])
        wait_for(got_y.at[it, pl.ds(0, count_y - 1)], y_s.at[it])
        wait_for(got_x.at[it, pl.ds(0, count_x - 1)], x_s.at[it])
        return c

    lax.fori_loop(0, ITERS, finish, 0)


def solve(acc, count_x, count_y):
    vmem = pl.BlockSpec(memory_space=pltpu.VMEM)
    field = jax.ShapeDtypeStruct((CZ, CX, CY), jnp.float32)
    cells = (CZ, CX, CY)

    def kernel(*refs):
        solve_kernel(count_x, count_y, *refs)

    return pl.pallas_call(
        kernel,
        out_shape=(field, field),
        in_specs=[vmem],
        out_specs=(vmem, vmem),
        scratch_shapes=[
            pltpu.VMEM((CZ + 2, CX, CY), jnp.float32),
            pltpu.VMEM(cells, jnp.float32),
            pltpu.VMEM(cells, jnp.float32),
            pltpu.VMEM(cells, jnp.float32),
            pltpu.VMEM(cells, jnp.float32),
            pltpu.VMEM((2, 2, CZ, LANES), jnp.float32),
            pltpu.VMEM((ITERS, 2, CZ, CY), jnp.float32),
            pltpu.VMEM((ITERS, 2, CZ, CY), jnp.float32),
            pltpu.VMEM((ITERS, 2, 8, LANES), jnp.float32),
            pltpu.VMEM((ITERS, 2, 3, 8, LANES), jnp.float32),
            pltpu.VMEM((ITERS, 8, LANES), jnp.float32),
            pltpu.VMEM((ITERS, 8, LANES), jnp.float32),
            pltpu.VMEM((ITERS, count_y, 8, LANES), jnp.float32),
            pltpu.VMEM((ITERS, count_x, 8, LANES), jnp.float32),
        ]
        + [pltpu.SemaphoreType.DMA((ITERS,))] * 8,
        compiler_params=pltpu.CompilerParams(
            collective_id=0, has_side_effects=True, vmem_limit_bytes=32 << 20
        ),
    )(acc)


def local(fractions, normals, point_cells, block_owner, block_tile, block_count):
    count_x, count_y = lax.axis_size("gx"), lax.axis_size("gy")
    devices = count_x * count_y
    blocks = fractions.shape[0]
    capacity = 2 * blocks // devices
    owner = block_owner[:, 0]
    index = jnp.arange(blocks, dtype=jnp.int32)
    earlier = (owner[:, None] == owner[None, :]) & (index[None, :] < index[:, None])
    slot = owner * capacity + jnp.sum(earlier.astype(jnp.int32), axis=1)
    packed = arrange(
        slot, block_tile, block_count, fractions, normals, point_cells, devices * capacity
    )
    packed = packed.reshape(devices, capacity, 8, POINTS)
    got = lax.all_to_all(packed, ("gx", "gy"), split_axis=0, concat_axis=0, tiled=True)
    got = got.reshape(devices * capacity, 8, POINTS)
    header = got[:, 7, :2].astype(jnp.int32)
    acc = splat(header[:, 0], header[:, 1], got)
    return solve(acc, count_x, count_y)


def solution(mesh):
    placed = (
        P(("gx", "gy"), None, None),
        P(("gx", "gy"), None, None),
        P(("gx", "gy"), None),
        P(("gx", "gy"), None),
        P(("gx", "gy")),
        P(("gx", "gy")),
    )
    return jax.shard_map(
        local,
        mesh=mesh,
        in_specs=placed,
        out_specs=(P(None, "gx", "gy"), P(None, "gx", "gy")),
        check_vma=False,
    )
```

time: 783 us -> 118 us (0.15)
  blocking collectives: 325 us -> 30.6 us
  other arithmetic: 133 us -> 1.7 us
  local copies, waits for them, and re-layouts: 133 us -> 6.44 us
  Pallas kernels: 0 us -> 77.9 us
  matrix products: 63.3 us -> 0 us
  starting transfers between devices: 55 us -> 0 us
  waiting for transfers between devices: 42.7 us -> 0 us
  loops' own time: 15.6 us -> 0 us
    psum x5 -> x0, blocking collectives: 325 us -> none  [the longest x3 193 us: squares(): return lax.psum(jnp.sum(residual * residual), ('gx', 'gy'))]
    pallas_call x0 -> x3, Pallas kernels: none -> 77.9 us  [the longest x1 62.3 us: solve(): pl.pallas_call(kernel, out_shape=(field, field), in_specs=[vmem], out_spe...]
    mul x10 -> x0, other arithmetic: 65.6 us -> none  [the longest x2 17.9 us: outer_pair(): return (first[:, :, None] * second[:, None, :]).reshape(points, CZ * TX)]
    dot_general x4 -> x0, matrix products: 63.3 us -> none  [the longest x2 36.5 us: splat_block(): jnp.dot(left.T, right, precision=lax.Precision.HIGHEST, preferred_element...]
    mul x6 -> x0, local copies, waits for them, and re-layouts: 54 us -> none  [outer_pair(): return (first[:, :, None] * second[:, None, :]).reshape(points, CZ * TX)]
    all_to_all x0 -> x1, blocking collectives: none -> 30.6 us  [local(): lax.all_to_all(packed, ('gx', 'gy'), split_axis=0, concat_axis=0, tiled=T...]
    all_to_all x4 -> x0, waiting for transfers between devices: 29.4 us -> none  [the longest x1 10.5 us: local(): lax.all_to_all(arrange(fractions), ('gx', 'gy'), split_axis=0, concat_axi...]
    ppermute x12 -> x0, starting transfers between devices: 28.1 us -> none  [the longest x6 18.5 us: with_halo(): lax.ppermute(lax.slice_in_dim(block, block.shape[dim] - width, None, axis...]
  transfers between devices with their start and end apart: 16 -> 0, of which waited for: 9 -> 0; matrix products, arithmetic and copies ran while one was open for 5% -> 0% of each run, Pallas kernels for 0% -> 0%
where the time goes in v1:
time: 118 us; the launch traced here: 117 us
  Pallas kernels  77.9 us (66%)
  blocking collectives  30.6 us (26%)
  local copies, waits for them, and re-layouts  6.44 us (5%)
  other arithmetic  1.7 us (1%)
    pallas_call x1, Pallas kernels, solve(): pl.pallas_call(kernel, out_shape=(field, field), in_specs=[vmem], out_spe...  62.3 us
    all_to_all x1, blocking collectives, local(): lax.all_to_all(packed, ('gx', 'gy'), split_axis=0, concat_axis=0, tiled=T...  30.6 us
    pallas_call x1, Pallas kernels, splat(): pl.pallas_call(splat_kernel, out_shape=jax.ShapeDtypeStruct((CX // TX, 2,...  13.9 us
    unnamed x10, local copies, waits for them, and re-layouts  6.22 us

profile of v1, /device:TPU:1, one launch (start us, length us, event | category | flops | bytes accessed | tf_op | source)
XLA Modules:
  0.0 117.4 jit_solution(10245827312900348887)
XLA Ops:
  0.6 0.9 convert_reduce_fusion
  1.5 0.7 multiply_add_fusion.slot_ref
  2.2 1.1 copy.12.frac_ref
  3.3 1.1 copy.13.norm_ref
  4.3 0.0 copy-start
  4.3 0.8 copy-done
  5.2 0.0 copy-start.1
  5.2 0.7 copy-done.1
  5.8 0.0 copy-start.2
  5.8 0.7 copy-done.2
  6.5 1.6 %shard_map.77 = f32[256,8,128]{2,1,0:T(8,128)S(1)} custom-call(s32[128]{0:T(128)S(1)} %multiply_add_fusion.slot_ref, s32[128]{0:T(128)S(1)} %copy-done.1, s32[128]{0:T(128)S(1)} %copy-done.2, f32[128,3,128]{2,1,0:T(4,128)S(1)} %copy.12.frac_ref, f32[128,3,128]{2,1,0:T(4,128)S(1)} %copy.13.norm_ref, s32[128,128]{1,0:T(8,128)S(1)} %copy-done), custom_call_target="tpu_custom_call" | custom-call | tf_op jit(solution)/shard_map/pallas_call | solution.py:42
  8.1 30.6 %all_to_all.5 = f32[128,2,8,128]{3,2,1,0:T(8,128)S(1)} all-to-all(f32[128,2,8,128]{3,2,1,0:T(8,128)S(1)} %bitcast.7), channel_id=1, replica_groups=mesh['gx'=16,'gy'=8] {'gx','gy'}, dimensions={0} | all-to-all | bytes 2097152 | tf_op jit(solution)/shard_map/all_to_all | solution.py:448
  38.8 0.1 slice_convert_fusion
  38.9 0.2 slice_reduce_fusion
  39.1 13.9 %shard_map.78.refs_0_ = f32[8,2,256,128]{3,2,1,0:T(8,128)S(1)} custom-call(s32[256]{0:T(256)S(1)} %get-tuple-element.3.tile_ref, s32[256]{0:T(256)S(1)} %get-tuple-element.2.count_ref, f32[256,8,128]{2,1,0:T(8,128)S(1)} %bitcast.6), custom_call_target="tpu_custom_call" | custom-call | tf_op jit(solution)/shard_map/pallas_call | solution.py:139
  53.1 62.3 %shard_map.79 = (f32[16,64,256]{2,1,0:T(8,128)S(1)}, f32[16,64,256]{2,1,0:T(8,128)S(1)}) custom-call(f32[8,2,256,128]{3,2,1,0:T(8,128)S(1)} %shard_map.78.refs_0_), custom_call_target="tpu_custom_call" | custom-call | tf_op jit(solution)/shard_map/pallas_call | solution.py:407
  115.4 1.0 copy.16
  116.4 1.0 copy.17
Async XLA Ops:
  4.3 0.8 copy-start
  5.2 0.7 copy-start.1
  5.8 0.7 copy-start.2

commit v2 on v1

--- a/solution.py
+++ b/solution.py
@@ -13,7 +13,9 @@
 POINTS = 128
 ITERS = 3
 LANES = 128
-GROUP = 4
+GROUP = 16
+SHIFT = 6.5
+TRUST = 100.0
 
 screen_weight = 4.0
 MESH = pl.DeviceIdType.MESH
@@ -105,14 +107,12 @@
     def gather(i, carry):
         used, empty = carry
         some = count_ref[i] > 0
-
-        @pl.when(some)
-        def _():
-            order[used] = i
-
+        order[used] = i
         return used + some.astype(jnp.int32), jnp.where(some, empty, i)
 
-    used, empty = lax.fori_loop(0, slots, gather, (jnp.int32(0), jnp.int32(0)))
+    used, empty = lax.fori_loop(
+        0, slots, gather, (jnp.int32(0), jnp.int32(0)), unroll=8
+    )
     for extra in range(GROUP):
         order[used + extra] = empty
 
@@ -432,6 +432,335 @@
     )(acc)
 
 
+def blend_kernel(
+    count_x, count_y,
+    acc_ref, x_ref, r_ref, flag_ref,
+    vs, dg, rim, sums,
+    row_out, row_in, col_out, col_in, part_y, part_x, got_y, got_x,
+    row_s, row_r, col_s, col_r, y_s, y_r, x_s, x_r,
+):
+    me_x, me_y = lax.axis_index("gx"), lax.axis_index("gy")
+
+    def at(dx, dy):
+        return (lax.rem(me_x + dx + count_x, count_x), lax.rem(me_y + dy + count_y, count_y))
+
+    barrier = pltpu.get_barrier_semaphore()
+
+    def greet_y(d, carry):
+        pl.semaphore_signal(barrier, inc=1, device_id=at(0, d), device_id_type=MESH)
+        return carry
+
+    def greet_x(d, carry):
+        pl.semaphore_signal(barrier, inc=1, device_id=at(d, 0), device_id_type=MESH)
+        return carry
+
+    lax.fori_loop(1, count_y, greet_y, 0)
+    lax.fori_loop(1, count_x, greet_x, 0)
+    for dx in (-1, 1):
+        for dy in (-1, 1):
+            pl.semaphore_signal(barrier, inc=1, device_id=at(dx, dy), device_id_type=MESH)
+
+    tiles_x = CX // TX
+    sub8 = lax.broadcasted_iota(jnp.int32, (8, LANES), 0)
+    lane8 = lax.broadcasted_iota(jnp.int32, (8, LANES), 1)
+    lane_half = lax.broadcasted_iota(jnp.int32, (CX, LANES), 1)
+    row_half = lax.broadcasted_iota(jnp.int32, (CX, LANES), 0)
+    plane8 = lax.rem(lane8, CZ)
+    zrow = lax.broadcasted_iota(jnp.int32, (CZ, CY), 0)
+    yrow = lax.broadcasted_iota(jnp.int32, (CZ, CY), 1)
+    zero8 = jnp.zeros((8, LANES), jnp.float32)
+
+    for k in range(ITERS):
+        vs[k, 0] = jnp.zeros((CX, CY), jnp.float32)
+        vs[k, CZ + 1] = jnp.zeros((CX, CY), jnp.float32)
+
+    def unfold(t, carry):
+        rows = pl.ds(pl.multiple_of(t * TX, TX), TX)
+        vs[0, 1 : CZ + 1, rows, :] = acc_ref[t, 0].T.reshape(CZ, TX, CY)
+        dg[:, rows, :] = (6.75 - SHIFT) + screen_weight * acc_ref[t, 1].T.reshape(CZ, TX, CY)
+        return carry
+
+    lax.fori_loop(0, tiles_x, unfold, 0)
+
+    def collect(z, t, left, right, west, east):
+        shift = z + CZ * t
+        mine = lane8 == shift
+        west = jnp.where(mine, pltpu.roll(left, shift, 1), west)
+        east = jnp.where(mine, pltpu.roll(right, lax.rem(shift + 1, LANES), 1), east)
+        return west, east
+
+    def first(z, carry):
+        west, east, norm = carry
+        for t in range(tiles_x):
+            left = vs[0, z + 1, 8 * t : 8 * t + 8, :LANES]
+            right = vs[0, z + 1, 8 * t : 8 * t + 8, LANES:]
+            west, east = collect(z, t, left, right, west, east)
+            norm = norm + left * left + right * right
+        return west, east, norm
+
+    west, east, norm = lax.fori_loop(0, CZ, first, (zero8, zero8, zero8))
+    sums[0] = norm
+    pl.semaphore_wait(barrier, (count_y - 1) + (count_x - 1) + 4)
+
+    def ask(target, src, dst, send, recv):
+        pltpu.make_async_remote_copy(
+            src_ref=src, dst_ref=dst, send_sem=send, recv_sem=recv,
+            device_id=target, device_id_type=MESH,
+        ).start()
+
+    def wait_for(ref, sem):
+        pltpu.make_async_copy(ref, ref, sem).wait()
+
+    def turn(it, carry):
+        west, east = carry
+        col_out[it, 0] = west
+        col_out[it, 1] = east
+        for dx in (-1, 1, 0):
+            ask(at(dx, -1), col_out.at[it, 0], col_in.at[it, 1, 1 - dx], col_s.at[it], col_r.at[it])
+            ask(at(dx, 1), col_out.at[it, 1], col_in.at[it, 0, 1 - dx], col_s.at[it], col_r.at[it])
+        row_out[it, 0] = vs[it, 1 : CZ + 1, 0, :]
+        row_out[it, 1] = vs[it, 1 : CZ + 1, CX - 1, :]
+        ask(at(-1, 0), row_out.at[it, 0], row_in.at[it, 1], row_s.at[it], row_r.at[it])
+        ask(at(1, 0), row_out.at[it, 1], row_in.at[it, 0], row_s.at[it], row_r.at[it])
+
+        def inner(z, c):
+            halves = []
+            for h in range(2):
+                cols = slice(h * LANES, (h + 1) * LANES)
+                u = vs[it, z, :, cols] + vs[it, z + 1, :, cols] + vs[it, z + 2, :, cols]
+                halves.append(
+                    u
+                    + jnp.where(row_half == 0, 0.0, pltpu.roll(u, 1, 0))
+                    + jnp.where(row_half == CX - 1, 0.0, pltpu.roll(u, CX - 1, 0))
+                )
+            left, right = halves
+            lr, rr = pltpu.roll(left, 1, 1), pltpu.roll(right, 1, 1)
+            ll, rl = pltpu.roll(left, LANES - 1, 1), pltpu.roll(right, LANES - 1, 1)
+            start, last = lane_half == 0, lane_half == LANES - 1
+            box_left = left + jnp.where(start, 0.0, lr) + jnp.where(last, rl, ll)
+            box_right = right + jnp.where(start, lr, rr) + jnp.where(last, 0.0, rl)
+            for h, box in ((0, box_left), (1, box_right)):
+                cols = slice(h * LANES, (h + 1) * LANES)
+                vs[it + 1, z + 1, :, cols] = dg[z, :, cols] * vs[it, z + 1, :, cols] - 0.25 * box
+            return c
+
+        lax.fori_loop(0, CZ, inner, 0)
+
+        wait_for(row_in.at[it], row_r.at[it])
+        for side, there in ((0, me_x > 0), (1, me_x < count_x - 1)):
+            near = row_in[it, side]
+            near = (
+                near
+                + jnp.where(zrow > 0, pltpu.roll(near, 1, 0), 0.0)
+                + jnp.where(zrow < CZ - 1, pltpu.roll(near, CZ - 1, 0), 0.0)
+            )
+            near = (
+                near
+                + jnp.where(yrow > 0, pltpu.roll(near, 1, 1), 0.0)
+                + jnp.where(yrow < CY - 1, pltpu.roll(near, CY - 1, 1), 0.0)
+            )
+            near = jnp.where(there, 0.25 * near, 0.0)
+            rim[side, 0] = near[:, :LANES]
+            rim[side, 1] = near[:, LANES:]
+        wait_for(col_in.at[it], col_r.at[it])
+
+        def column(side, there):
+            def summed(k, ok):
+                col = col_in[it, side, k]
+                col = (
+                    col
+                    + jnp.where(plane8 > 0, pltpu.roll(col, 1, 1), 0.0)
+                    + jnp.where(plane8 < CZ - 1, pltpu.roll(col, LANES - 1, 1), 0.0)
+                )
+                return jnp.where(ok, 0.25 * col, 0.0)
+
+            mid = summed(1, there)
+            low = summed(0, jnp.logical_and(there, me_x > 0))
+            high = summed(2, jnp.logical_and(there, me_x < count_x - 1))
+
+            def down(v):
+                return pltpu.roll(v, 1, 0)
+
+            def up(v):
+                return pltpu.roll(v, 7, 0)
+
+            before = jnp.where(lane8 < CZ, pltpu.roll(down(low), CZ, 1), pltpu.roll(down(mid), CZ, 1))
+            before = jnp.where(sub8 == 0, before, down(mid))
+            after = jnp.where(
+                lane8 >= LANES - CZ,
+                pltpu.roll(up(high), LANES - CZ, 1),
+                pltpu.roll(up(mid), LANES - CZ, 1),
+            )
+            after = jnp.where(sub8 == 7, after, up(mid))
+            return before + mid + after
+
+        west_in = column(0, me_y > 0)
+        east_in = column(1, me_y < count_y - 1)
+
+        def edge(z, carry):
+            west, east, cross, norm = carry
+            for t in range(tiles_x):
+                rows = slice(8 * t, 8 * t + 8)
+                shift = z + CZ * t
+                fixes = [
+                    jnp.where(lane8 == 0, pltpu.roll(west_in, lax.rem(2 * LANES - shift, LANES), 1), 0.0),
+                    jnp.where(lane8 == LANES - 1, pltpu.roll(east_in, 2 * LANES - 1 - shift - LANES, 1), 0.0),
+                ]
+                made = []
+                for h in range(2):
+                    cols = slice(h * LANES, (h + 1) * LANES)
+                    value = vs[it + 1, z + 1, rows, cols] - fixes[h]
+                    if t == 0:
+                        value = value - jnp.where(sub8 == 0, rim[0, h, pl.ds(z, 1), :], 0.0)
+                    if t == tiles_x - 1:
+                        value = value - jnp.where(sub8 == 7, rim[1, h, pl.ds(z, 1), :], 0.0)
+                    vs[it + 1, z + 1, rows, cols] = value
+                    cross = cross + value * vs[it, z + 1, rows, cols]
+                    norm = norm + value * value
+                    made.append(value)
+                west, east = collect(z, t, made[0], made[1], west, east)
+            return west, east, cross, norm
+
+        west, east, cross, norm = lax.fori_loop(0, CZ, edge, (zero8, zero8, zero8, zero8))
+        sums[2 * it + 1] = cross
+        sums[2 * it + 2] = norm
+        return west, east
+
+    lax.fori_loop(0, ITERS, turn, (west, east))
+
+    mine = zero8
+    for k in range(2 * ITERS + 1):
+        mine = jnp.where(sub8 == k, jnp.sum(sums[k], axis=0, keepdims=True), mine)
+    part_y[...] = mine
+    got_y[me_y] = mine
+
+    def send_y(d, c):
+        ask(at(0, d), part_y, got_y.at[me_y], y_s, y_r)
+        return c
+
+    lax.fori_loop(1, count_y, send_y, 0)
+    wait_for(got_y.at[pl.ds(0, count_y - 1)], y_r)
+
+    def total_of(parts):
+        total = parts[0]
+        for k in range(1, parts.shape[0]):
+            total = total + parts[k]
+        return total
+
+    mine = total_of(got_y)
+    part_x[...] = mine
+    got_x[me_x] = mine
+
+    def send_x(d, c):
+        ask(at(d, 0), part_x, got_x.at[me_x], x_s, x_r)
+        return c
+
+    lax.fori_loop(1, count_x, send_x, 0)
+    wait_for(got_x.at[pl.ds(0, count_x - 1)], x_r)
+    total = jnp.sum(total_of(got_x), axis=1, keepdims=True)
+    moment = [total[k : k + 1] for k in range(2 * ITERS + 1)]
+
+    good = jnp.ones((1, 1), jnp.float32)
+
+    def product(a, b, good):
+        value, size = 0.0, 0.0
+        for d in range(len(a) + len(b) - 1):
+            pairs = [a[i] * b[d - i] for i in range(len(a)) if 0 <= d - i < len(b)]
+            both = pairs[0]
+            bulk = jnp.abs(pairs[0])
+            for pair in pairs[1:]:
+                both = both + pair
+                bulk = bulk + jnp.abs(pair)
+            value = value + both * moment[d]
+            size = size + bulk * jnp.abs(moment[d])
+        return value, jnp.where(size <= TRUST * value, good, 0.0)
+
+    def image(a):
+        padded = [SHIFT * c for c in a] + [None]
+        return [
+            (padded[i] if i == 0 else a[i - 1] if i == len(a) else padded[i] + a[i - 1])
+            for i in range(len(a) + 1)
+        ]
+
+    def plus(a, factor, b):
+        longest = max(len(a), len(b))
+        made = []
+        for i in range(longest):
+            if i >= len(a):
+                made.append(factor * b[i])
+            elif i >= len(b):
+                made.append(a[i])
+            else:
+                made.append(a[i] + factor * b[i])
+        return made
+
+    one = jnp.ones((1, 1), jnp.float32)
+    residual, direction, answer = [one], [one], []
+    gamma, good = product(residual, residual, good)
+    for it in range(ITERS):
+        curve, good = product(direction, image(direction), good)
+        alpha = gamma / curve
+        answer = plus(answer, alpha, direction)
+        residual = plus(residual, -alpha, image(direction))
+        fresh, good = product(residual, residual, good)
+        direction = plus(residual, fresh / gamma, direction)
+        gamma = fresh
+    flag_ref[...] = jnp.broadcast_to(good, (8, LANES))
+
+    def combine(z, c):
+        for h in range(2):
+            cols = slice(h * LANES, (h + 1) * LANES)
+            fields = [vs[k, z + 1, :, cols] for k in range(ITERS + 1)]
+            x_ref[z, :, cols] = sum(answer[k] * fields[k] for k in range(ITERS))
+            r_ref[z, :, cols] = sum(residual[k] * fields[k] for k in range(ITERS + 1))
+        return c
+
+    lax.fori_loop(0, CZ, combine, 0)
+
+    def finish(it, c):
+        wait_for(row_out.at[it], row_s.at[it])
+        wait_for(col_in.at[it], col_s.at[it])
+        return c
+
+    lax.fori_loop(0, ITERS, finish, 0)
+    wait_for(got_y.at[pl.ds(0, count_y - 1)], y_s)
+    wait_for(got_x.at[pl.ds(0, count_x - 1)], x_s)
+
+
+def blend(acc, count_x, count_y):
+    vmem = pl.BlockSpec(memory_space=pltpu.VMEM)
+    field = jax.ShapeDtypeStruct((CZ, CX, CY), jnp.float32)
+
+    def kernel(*refs):
+        blend_kernel(count_x, count_y, *refs)
+
+    return pl.pallas_call(
+        kernel,
+        out_shape=(field, field, jax.ShapeDtypeStruct((8, LANES), jnp.float32)),
+        in_specs=[vmem],
+        out_specs=(vmem, vmem, vmem),
+        scratch_shapes=[
+            pltpu.VMEM((ITERS + 1, CZ + 2, CX, CY), jnp.float32),
+            pltpu.VMEM((CZ, CX, CY), jnp.float32),
+            pltpu.VMEM((2, 2, CZ, LANES), jnp.float32),
+            pltpu.VMEM((2 * ITERS + 1, 8, LANES), jnp.float32),
+            pltpu.VMEM((ITERS, 2, CZ, CY), jnp.float32),
+            pltpu.VMEM((ITERS, 2, CZ, CY), jnp.float32),
+            pltpu.VMEM((ITERS, 2, 8, LANES), jnp.float32),
+            pltpu.VMEM((ITERS, 2, 3, 8, LANES), jnp.float32),
+            pltpu.VMEM((8, LANES), jnp.float32),
+            pltpu.VMEM((8, LANES), jnp.float32),
+            pltpu.VMEM((count_y, 8, LANES), jnp.float32),
+            pltpu.VMEM((count_x, 8, LANES), jnp.float32),
+        ]
+        + [pltpu.SemaphoreType.DMA((ITERS,))] * 4
+        + [pltpu.SemaphoreType.DMA] * 4,
+        compiler_params=pltpu.CompilerParams(
+            collective_id=1, has_side_effects=True, vmem_limit_bytes=32 << 20
+        ),
+    )(acc)
+
+
 def local(fractions, normals, point_cells, block_owner, block_tile, block_count):
     count_x, count_y = lax.axis_size("gx"), lax.axis_size("gy")
     devices = count_x * count_y
@@ -449,7 +778,13 @@
     got = got.reshape(devices * capacity, 8, POINTS)
     header = got[:, 7, :2].astype(jnp.int32)
     acc = splat(header[:, 0], header[:, 1], got)
-    return solve(acc, count_x, count_y)
+    x, r, flag = blend(acc, count_x, count_y)
+    return lax.cond(
+        flag[0, 0] > 0.5,
+        lambda acc, x, r: (x, r),
+        lambda acc, x, r: tuple(solve(acc, count_x, count_y)),
+        acc, x, r,
+    )
 
 
 def solution(mesh):

time: 118 us -> 90.2 us (0.76)
  Pallas kernels: 77.9 us -> 49.2 us
    pallas_call x1, Pallas kernels: 62.3 us -> 39.8 us  [blend(): pl.pallas_call(kernel, out_shape=(field, field, jax.ShapeDtypeStruct((8,...]
    pallas_call x1, Pallas kernels: 13.9 us -> 7.78 us  [splat(): pl.pallas_call(splat_kernel, out_shape=jax.ShapeDtypeStruct((CX // TX, 2,...]
where the time goes in v2:
time: 90.2 us; the launch traced here: 89.9 us
  Pallas kernels  49.2 us (55%)
  blocking collectives  30.6 us (34%)
  local copies, waits for them, and re-layouts  6.95 us (8%)
  other arithmetic  1.7 us (2%)
  between operations  1.34 us (1%)
    pallas_call x1, Pallas kernels, blend(): pl.pallas_call(kernel, out_shape=(field, field, jax.ShapeDtypeStruct((8,...  39.8 us
    all_to_all x1, blocking collectives, local(): lax.all_to_all(packed, ('gx', 'gy'), split_axis=0, concat_axis=0, tiled=T...  30.6 us
    pallas_call x1, Pallas kernels, splat(): pl.pallas_call(splat_kernel, out_shape=jax.ShapeDtypeStruct((CX // TX, 2,...  7.78 us
    unnamed x10, local copies, waits for them, and re-layouts  6.22 us

profile of v2, /device:TPU:1, one launch (start us, length us, event | category | flops | bytes accessed | tf_op | source)
XLA Modules:
  0.0 89.9 jit_solution(16633544519262294771)
XLA Ops:
  0.6 0.9 convert_reduce_fusion
  1.5 0.7 multiply_add_fusion.slot_ref
  2.2 1.1 %copy.16.frac_ref = f32[128,3,128]{2,1,0:T(4,128)S(1)} copy(f32[128,3,128]{2,0,1:T(8,128)} %param.8) | data formatting | bytes 393216 | tf_op args[0]
  3.3 1.1 %copy.17.norm_ref = f32[128,3,128]{2,1,0:T(4,128)S(1)} copy(f32[128,3,128]{2,0,1:T(8,128)} %param.9) | data formatting | bytes 393216 | tf_op args[1]
  4.3 0.0 copy-start
  4.3 0.8 copy-done
  5.2 0.0 copy-start.1
  5.2 0.7 copy-done.1
  5.8 0.0 copy-start.2
  5.8 0.7 copy-done.2
  6.5 1.6 %shard_map.81 = f32[256,8,128]{2,1,0:T(8,128)S(1)} custom-call(s32[128]{0:T(128)S(1)} %multiply_add_fusion.slot_ref, s32[128]{0:T(128)S(1)} %copy-done.1, s32[128]{0:T(128)S(1)} %copy-done.2, f32[128,3,128]{2,1,0:T(4,128)S(1)} %copy.16.frac_ref, f32[128,3,128]{2,1,0:T(4,128)S(1)} %copy.17.norm_ref, s32[128,128]{1,0:T(8,128)S(1)} %copy-done), custom_call_target="tpu_custom_call" | custom-call | tf_op jit(solution)/shard_map/pallas_call | solution.py:44
  8.1 30.6 %all_to_all.5 = f32[128,2,8,128]{3,2,1,0:T(8,128)S(1)} all-to-all(f32[128,2,8,128]{3,2,1,0:T(8,128)S(1)} %bitcast.8), channel_id=1, replica_groups=mesh['gx'=16,'gy'=8] {'gx','gy'}, dimensions={0} | all-to-all | bytes 2097152 | tf_op jit(solution)/shard_map/all_to_all | solution.py:777
  38.8 0.1 slice_convert_fusion
  38.9 0.2 slice_reduce_fusion
  39.1 7.8 %shard_map.82.refs_0_ = f32[8,2,256,128]{3,2,1,0:T(8,128)S(1)} custom-call(s32[256]{0:T(256)S(1)} %get-tuple-element.20.tile_ref, s32[256]{0:T(256)S(1)} %get-tuple-element.19.count_ref, f32[256,8,128]{2,1,0:T(8,128)S(1)} %bitcast.7), custom_call_target="tpu_custom_call" | custom-call | tf_op jit(solution)/shard_map/pallas_call | solution.py:139
  46.9 39.8 %shard_map.83 = (f32[16,64,256]{2,1,0:T(8,128)S(1)}, f32[16,64,256]{2,1,0:T(8,128)S(1)}, f32[8,128]{1,0:T(8,128)S(1)}) custom-call(f32[8,2,256,128]{3,2,1,0:T(8,128)S(1)} %shard_map.82.refs_0_), custom_call_target="tpu_custom_call" | custom-call | tf_op jit(solution)/shard_map/pallas_call | solution.py:737
  86.8 0.5 slice.15
  88.0 1.0 %copy.24 = f32[16,64,256]{2,1,0:T(8,128)} copy(f32[16,64,256]{2,1,0:T(8,128)S(1)} %get-tuple-element.27) | data formatting | bytes 2097152
  88.9 1.0 %copy.25 = f32[16,64,256]{2,1,0:T(8,128)} copy(f32[16,64,256]{2,1,0:T(8,128)S(1)} %get-tuple-element.28) | data formatting | bytes 2097152
  (1 shorter events, 0.0 us)
Async XLA Ops:
  4.3 0.8 copy-start
  5.2 0.7 copy-start.1
  5.8 0.7 copy-start.2

commit v3 on v2

--- a/solution.py
+++ b/solution.py
@@ -13,7 +13,7 @@
 POINTS = 128
 ITERS = 3
 LANES = 128
-GROUP = 16
+GROUP = 32
 SHIFT = 6.5
 TRUST = 100.0
 
@@ -21,33 +21,135 @@
 MESH = pl.DeviceIdType.MESH
 
 
-def arrange_kernel(slot_ref, tile_ref, count_ref, frac_ref, norm_ref, cell_ref, out_ref):
-    blocks = frac_ref.shape[0]
+def route_kernel(
+    count_x, count_y,
+    tile_in, count_in, owner_in, frac_in, norm_in, cell_in, out_ref,
+    tile_ref, count_ref, owner_ref, frac_ref, norm_ref, cell_ref,
+    send, index_v, index_s, load_sem, copy_sem, send_sem, recv_sem,
+):
+    devices = count_x * count_y
+    blocks = cell_ref.shape[0]
+    loads = [
+        pltpu.make_async_copy(source, target, load_sem.at[k])
+        for k, (source, target) in enumerate(
+            (
+                (owner_in, owner_ref),
+                (tile_in, tile_ref),
+                (count_in, count_ref),
+                (frac_in, frac_ref),
+                (norm_in, norm_ref),
+                (cell_in, cell_ref),
+            )
+        )
+    ]
+    for load in loads:
+        load.start()
+    me = lax.axis_index("gx") * count_y + lax.axis_index("gy")
+
+    def place(d):
+        flat = lax.rem(me + d, devices)
+        return flat, (flat // count_y, lax.rem(flat, count_y))
+
+    barrier = pltpu.get_barrier_semaphore()
+
+    def greet(d, carry):
+        pl.semaphore_signal(barrier, inc=1, device_id=place(d)[1], device_id_type=MESH)
+        return carry
+
+    lax.fori_loop(1, devices, greet, 0)
+
+    loads[0].wait()
+    owner = jnp.broadcast_to(owner_ref[...], (devices, blocks)).T
+    block = lax.broadcasted_iota(jnp.int32, (blocks, devices), 0)
+    named = owner == lax.broadcasted_iota(jnp.int32, (blocks, devices), 1)
+    first = jnp.min(jnp.where(named, block, blocks), axis=0, keepdims=True)
+    last = jnp.max(jnp.where(named, block, -1), axis=0, keepdims=True)
+    sub = lax.broadcasted_iota(jnp.int32, (8, devices), 0)
+    index_v[...] = jnp.where(
+        sub == 0,
+        first,
+        jnp.where(
+            sub == 1,
+            last,
+            jnp.where(
+                sub == 2,
+                (last >= 0).astype(jnp.int32),
+                (last > first).astype(jnp.int32),
+            ),
+        ),
+    )
+    fetch = pltpu.make_async_copy(index_v, index_s, copy_sem)
+    fetch.start()
+    for load in loads[1:]:
+        load.wait()
+    fetch.wait()
+
     lane = lax.broadcasted_iota(jnp.int32, (1, LANES), 1)
-    out_ref[...] = jnp.zeros_like(out_ref)
-
-    def place(k, carry):
-        slot = slot_ref[k]
-        out_ref[slot, 0:3, :] = frac_ref[k]
-        out_ref[slot, 3:6, :] = norm_ref[k]
-        out_ref[slot, 6:7, :] = cell_ref[pl.ds(k, 1), :].astype(jnp.float32)
-        header = jnp.where(lane == 0, tile_ref[k], jnp.where(lane == 1, count_ref[k], 0))
-        out_ref[slot, 7:8, :] = header.astype(jnp.float32)
-        return carry
-
-    lax.fori_loop(0, blocks, place, 0)
-
-
-def arrange(slot, tile, count, fractions, normals, cells, slots):
-    smem = pl.BlockSpec(memory_space=pltpu.SMEM)
-    vmem = pl.BlockSpec(memory_space=pltpu.VMEM)
+
+    def fill(o, carry):
+        for c in range(2):
+            k = jnp.minimum(jnp.maximum(index_s[c, o], 0), blocks - 1)
+            there = index_s[2 + c, o]
+            slot = 2 * o + c
+            for axis in range(3):
+                send[slot, axis : axis + 1, :] = frac_ref[axis, pl.ds(k, 1), :]
+                send[slot, 3 + axis : 4 + axis, :] = norm_ref[axis, pl.ds(k, 1), :]
+            send[slot, 6:7, :] = cell_ref[pl.ds(k, 1), :].astype(jnp.float32)
+            header = jnp.where(lane == 0, tile_ref[k], jnp.where(lane == 1, count_ref[k] * there, 0))
+            send[slot, 7:8, :] = header.astype(jnp.float32)
+        return carry
+
+    lax.fori_loop(0, devices, fill, 0, unroll=4)
+    keep = pltpu.make_async_copy(
+        send.at[pl.ds(2 * me, 2)], out_ref.at[pl.ds(2 * me, 2)], copy_sem
+    )
+    keep.start()
+    pl.semaphore_wait(barrier, devices - 1)
+
+    def ship(d, carry):
+        flat, target = place(d)
+        pltpu.make_async_remote_copy(
+            src_ref=send.at[pl.ds(2 * flat, 2)],
+            dst_ref=out_ref.at[pl.ds(2 * me, 2)],
+            send_sem=send_sem, recv_sem=recv_sem,
+            device_id=target, device_id_type=MESH,
+        ).start()
+        return carry
+
+    lax.fori_loop(1, devices, ship, 0)
+    keep.wait()
+    most = pl.ds(0, 2 * (devices - 1))
+    pltpu.make_async_copy(out_ref.at[most], out_ref.at[most], recv_sem).wait()
+    pltpu.make_async_copy(send.at[most], send.at[most], send_sem).wait()
+
+
+def route(tile, count, owner, fractions, normals, cells, count_x, count_y):
+    slots = 2 * count_x * count_y
+    operands = (tile, count, owner, fractions, normals, cells)
+
+    def kernel(*refs):
+        route_kernel(count_x, count_y, *refs)
+
     return pl.pallas_call(
-        arrange_kernel,
+        kernel,
         out_shape=jax.ShapeDtypeStruct((slots, 8, LANES), jnp.float32),
-        in_specs=[smem, smem, smem, vmem, vmem, vmem],
-        out_specs=vmem,
-        compiler_params=pltpu.CompilerParams(vmem_limit_bytes=16 << 20),
-    )(slot, tile, count, fractions, normals, cells)
+        in_specs=[pl.BlockSpec(memory_space=pl.ANY)] * 6,
+        out_specs=pl.BlockSpec(memory_space=pl.ANY),
+        scratch_shapes=[pltpu.SMEM(tile.shape, tile.dtype), pltpu.SMEM(count.shape, count.dtype)]
+        + [pltpu.VMEM(one.shape, one.dtype) for one in operands[2:]]
+        + [
+            pltpu.VMEM((slots, 8, LANES), jnp.float32),
+            pltpu.VMEM((8, LANES), jnp.int32),
+            pltpu.SMEM((8, LANES), jnp.int32),
+            pltpu.SemaphoreType.DMA((6,)),
+            pltpu.SemaphoreType.DMA,
+            pltpu.SemaphoreType.DMA,
+            pltpu.SemaphoreType.DMA,
+        ],
+        compiler_params=pltpu.CompilerParams(
+            collective_id=2, has_side_effects=True, vmem_limit_bytes=56 << 20
+        ),
+    )(*operands)
 
 
 def split(value):
@@ -66,47 +168,68 @@
 
 def splat_tile(block, count):
     lane = lax.broadcasted_iota(jnp.int32, (1, POINTS), 1)
-    valid = lane < count
     cell = block[6:7]
     remains = jnp.floor((cell + 0.5) * (1.0 / (CZ - 1)))
     plane = cell - remains * (CZ - 1)
     row = jnp.floor((remains + 0.5) * (1.0 / (TY - 1)))
     column = remains - row * (TY - 1)
-    row = jnp.where(valid, row, -4.0)
+    row = jnp.where(lane < count, row, -4.0)
     wx, sx = taps(row, block[0:1], TX)
     wy, sy = taps(column, block[1:2], TY)
-    wz, sz = taps(plane, block[2:3], CZ)
-    sx = sx * block[3:4]
     sy = sy * block[4:5]
-    tx = wx * block[5:6]
-    first = jnp.concatenate(
-        [wz[z : z + 1] * sx + sz[z : z + 1] * tx for z in range(CZ)], axis=0
+    fz = block[2:3]
+    level = block[3:4] * sx
+    rise = block[5:6] * wx
+    pairs = (
+        ((1.0 - fz) * level - rise, fz * level + rise),
+        ((1.0 - fz) * wx, fz * wx),
     )
-    second = jnp.concatenate([wz[z : z + 1] * wx for z in range(CZ)], axis=0)
-    big = jnp.concatenate([first, second], axis=1)
+    at = jnp.broadcast_to(plane, (2 * TX, POINTS)).astype(jnp.bfloat16)
+    place = (lax.broadcasted_iota(jnp.int32, (2 * TX, POINTS), 0) // TX).astype(jnp.float32).astype(jnp.bfloat16)
+    offset = at - place
+    zero = jnp.zeros((2 * TX, POINTS), jnp.bfloat16)
+    high, low = [], []
+    for lower, upper in pairs:
+        lower = split(jnp.concatenate([lower, lower], axis=0))
+        upper = split(jnp.concatenate([upper, upper], axis=0))
+        for kept, under, over in zip((high, low), lower, upper):
+            kept.append(
+                jnp.concatenate(
+                    [
+                        jnp.where(offset == 2 * j, under, jnp.where(offset == 2 * j - 1, over, zero))
+                        for j in range(CZ // 2)
+                    ],
+                    axis=0,
+                )
+            )
+    big_high = jnp.concatenate(high, axis=1)
+    big_low = jnp.concatenate(low, axis=1)
     top = jnp.concatenate([wy, sy], axis=1)
     low = jnp.concatenate([jnp.zeros_like(wy), wy], axis=1)
-    small = jnp.concatenate([top, low], axis=0)
-    big_high, big_low = split(big)
-    small_high, small_low = split(small)
-    dims = (((1,), (1,)), ((), ()))
+    small_high, small_low = split(jnp.concatenate([top, low], axis=0))
     both = lax.dot_general(
         jnp.concatenate([small_high, small_low], axis=0),
-        big_high,
-        dims,
+        jnp.concatenate([big_high, big_low], axis=0),
+        (((1,), (1,)), ((), ())),
         preferred_element_type=jnp.float32,
     )
-    rest = lax.dot_general(small_high, big_low, dims, preferred_element_type=jnp.float32)
-    return both[: 2 * TY] + both[2 * TY :] + rest
-
-
-def splat_kernel(tile_ref, count_ref, blocks_ref, acc_ref, order):
+    return both[: 2 * TY, :POINTS] + both[2 * TY :, :POINTS] + both[: 2 * TY, POINTS:]
+
+
+def splat_kernel(blocks_ref, acc_ref, blocks, header_v, header_s, order, sem):
     slots = blocks_ref.shape[0]
+    load = pltpu.make_async_copy(blocks_ref, blocks, sem)
+    load.start()
     acc_ref[...] = jnp.zeros_like(acc_ref)
+    load.wait()
+    header_v[...] = blocks[:, 7, :].T[:8].astype(jnp.int32)
+    fetch = pltpu.make_async_copy(header_v, header_s, sem)
+    fetch.start()
+    fetch.wait()
 
     def gather(i, carry):
         used, empty = carry
-        some = count_ref[i] > 0
+        some = header_s[1, i] > 0
         order[used] = i
         return used + some.astype(jnp.int32), jnp.where(some, empty, i)
 
@@ -120,7 +243,7 @@
         made = []
         for u in range(GROUP):
             slot = order[j * GROUP + u]
-            made.append((tile_ref[slot], splat_tile(blocks_ref[slot], count_ref[slot])))
+            made.append((header_s[0, slot], splat_tile(blocks[slot], header_s[1, slot])))
         tiles_y = CY // TY
         for tile, values in made:
             x = tile // tiles_y
@@ -132,18 +255,22 @@
     lax.fori_loop(0, (used + GROUP - 1) // GROUP, work, 0)
 
 
-def splat(tile, count, blocks):
+def splat(blocks):
     slots = blocks.shape[0]
-    smem = pl.BlockSpec(memory_space=pltpu.SMEM)
-    vmem = pl.BlockSpec(memory_space=pltpu.VMEM)
     return pl.pallas_call(
         splat_kernel,
         out_shape=jax.ShapeDtypeStruct((CX // TX, 2, CY, CZ * TX), jnp.float32),
-        in_specs=[smem, smem, vmem],
-        out_specs=vmem,
-        scratch_shapes=[pltpu.SMEM((slots + GROUP,), jnp.int32)],
+        in_specs=[pl.BlockSpec(memory_space=pl.ANY)],
+        out_specs=pl.BlockSpec(memory_space=pltpu.VMEM),
+        scratch_shapes=[
+            pltpu.VMEM(blocks.shape, blocks.dtype),
+            pltpu.VMEM((8, slots), jnp.int32),
+            pltpu.SMEM((8, slots), jnp.int32),
+            pltpu.SMEM((slots + GROUP,), jnp.int32),
+            pltpu.SemaphoreType.DMA,
+        ],
         compiler_params=pltpu.CompilerParams(vmem_limit_bytes=24 << 20),
-    )(tile, count, blocks)
+    )(blocks)
 
 
 def fold(value):
@@ -498,7 +625,7 @@
             norm = norm + left * left + right * right
         return west, east, norm
 
-    west, east, norm = lax.fori_loop(0, CZ, first, (zero8, zero8, zero8))
+    west, east, norm = lax.fori_loop(0, CZ, first, (zero8, zero8, zero8), unroll=4)
     sums[0] = norm
     pl.semaphore_wait(barrier, (count_y - 1) + (count_x - 1) + 4)
 
@@ -544,7 +671,7 @@
                 vs[it + 1, z + 1, :, cols] = dg[z, :, cols] * vs[it, z + 1, :, cols] - 0.25 * box
             return c
 
-        lax.fori_loop(0, CZ, inner, 0)
+        lax.fori_loop(0, CZ, inner, 0, unroll=4)
 
         wait_for(row_in.at[it], row_r.at[it])
         for side, there in ((0, me_x > 0), (1, me_x < count_x - 1)):
@@ -621,7 +748,7 @@
                 west, east = collect(z, t, made[0], made[1], west, east)
             return west, east, cross, norm
 
-        west, east, cross, norm = lax.fori_loop(0, CZ, edge, (zero8, zero8, zero8, zero8))
+        west, east, cross, norm = lax.fori_loop(0, CZ, edge, (zero8, zero8, zero8, zero8), unroll=4)
         sums[2 * it + 1] = cross
         sums[2 * it + 2] = norm
         return west, east
@@ -705,7 +832,7 @@
         fresh, good = product(residual, residual, good)
         direction = plus(residual, fresh / gamma, direction)
         gamma = fresh
-    flag_ref[...] = jnp.broadcast_to(good, (8, LANES))
+    flag_ref[...] = good
 
     def combine(z, c):
         for h in range(2):
@@ -715,7 +842,7 @@
             r_ref[z, :, cols] = sum(residual[k] * fields[k] for k in range(ITERS + 1))
         return c
 
-    lax.fori_loop(0, CZ, combine, 0)
+    lax.fori_loop(0, CZ, combine, 0, unroll=2)
 
     def finish(it, c):
         wait_for(row_out.at[it], row_s.at[it])
@@ -736,7 +863,7 @@
 
     return pl.pallas_call(
         kernel,
-        out_shape=(field, field, jax.ShapeDtypeStruct((8, LANES), jnp.float32)),
+        out_shape=(field, field, jax.ShapeDtypeStruct((1, 1), jnp.float32)),
         in_specs=[vmem],
         out_specs=(vmem, vmem, vmem),
         scratch_shapes=[
@@ -763,21 +890,17 @@
 
 def local(fractions, normals, point_cells, block_owner, block_tile, block_count):
     count_x, count_y = lax.axis_size("gx"), lax.axis_size("gy")
-    devices = count_x * count_y
-    blocks = fractions.shape[0]
-    capacity = 2 * blocks // devices
-    owner = block_owner[:, 0]
-    index = jnp.arange(blocks, dtype=jnp.int32)
-    earlier = (owner[:, None] == owner[None, :]) & (index[None, :] < index[:, None])
-    slot = owner * capacity + jnp.sum(earlier.astype(jnp.int32), axis=1)
-    packed = arrange(
-        slot, block_tile, block_count, fractions, normals, point_cells, devices * capacity
+    got = route(
+        block_tile,
+        block_count,
+        block_owner.reshape(1, -1),
+        jnp.transpose(fractions, (1, 0, 2)),
+        jnp.transpose(normals, (1, 0, 2)),
+        point_cells,
+        count_x,
+        count_y,
     )
-    packed = packed.reshape(devices, capacity, 8, POINTS)
-    got = lax.all_to_all(packed, ("gx", "gy"), split_axis=0, concat_axis=0, tiled=True)
-    got = got.reshape(devices * capacity, 8, POINTS)
-    header = got[:, 7, :2].astype(jnp.int32)
-    acc = splat(header[:, 0], header[:, 1], got)
+    acc = splat(got)
     x, r, flag = blend(acc, count_x, count_y)
     return lax.cond(
         flag[0, 0] > 0.5,

time: 90.2 us -> 77.1 us (0.85)
  blocking collectives: 30.6 us -> 0 us
  Pallas kernels: 49.2 us -> 71.7 us
  local copies, waits for them, and re-layouts: 6.95 us -> 3.78 us
  other arithmetic: 1.7 us -> 0 us
    all_to_all x1 -> x0, blocking collectives: 30.6 us -> none  [local(): lax.all_to_all(packed, ('gx', 'gy'), split_axis=0, concat_axis=0, tiled=T...]
    pallas_call x2, Pallas kernels: 41.5 us -> 64 us  [the longest x1 36.3 us: blend(): pl.pallas_call(kernel, out_shape=(field, field, jax.ShapeDtypeStruct((1,...]
    unnamed x10 -> x6, local copies, waits for them, and re-layouts: 6.22 us -> 3.78 us
where the time goes in v3:
time: 77.1 us; the launch traced here: 76.9 us
  Pallas kernels  71.7 us (93%)
  local copies, waits for them, and re-layouts  3.78 us (5%)
  between operations  1.36 us (2%)
    pallas_call x1, Pallas kernels, blend(): pl.pallas_call(kernel, out_shape=(field, field, jax.ShapeDtypeStruct((1,...  36.3 us
    pallas_call x1, Pallas kernels, route(): pl.pallas_call(kernel, out_shape=jax.ShapeDtypeStruct((slots, 8, LANES),...  27.7 us
    pallas_call x1, Pallas kernels, splat(): pl.pallas_call(splat_kernel, out_shape=jax.ShapeDtypeStruct((CX // TX, 2,...  7.73 us
    unnamed x6, local copies, waits for them, and re-layouts  3.78 us

profile of v3, /device:TPU:1, one launch (start us, length us, event | category | flops | bytes accessed | tf_op | source)
XLA Modules:
  0.0 76.9 jit_solution(2654839962104009874)
XLA Ops:
  0.6 27.7 %shard_map.81.blocks_ref = f32[256,8,128]{2,1,0:T(8,128)} custom-call(s32[128]{0:T(128)} %refs_0_.2, s32[128]{0:T(128)} %refs_1_.1, s32[1,128]{1,0:T(1,128)} %bitcast.6, f32[3,128,128]{2,1,0:T(8,128)} %bitcast.4, f32[3,128,128]{2,1,0:T(8,128)} %bitcast.5, s32[128,128]{1,0:T(8,128)} %refs_5_.1), custom_call_target="tpu_custom_call" | custom-call | tf_op jit(solution)/shard_map/pallas_call | solution.py:133
  28.3 0.0 copy-start
  28.4 1.2 %copy-done = f32[256,8,128]{2,1,0:T(8,128)S(1)} copy-done((f32[256,8,128]{2,1,0:T(8,128)S(1)}, f32[256,8,128]{2,1,0:T(8,128)}, u32[]{:S(2)}) %copy-start) | copy-done | bytes 1048600
  29.6 7.7 %shard_map.82.refs_0_ = f32[8,2,256,128]{3,2,1,0:T(8,128)S(1)} custom-call(f32[256,8,128]{2,1,0:T(8,128)S(1)} %copy-done), custom_call_target="tpu_custom_call" | custom-call | tf_op jit(solution)/shard_map/pallas_call | solution.py:260
  37.3 36.3 %shard_map.83 = (f32[16,64,256]{2,1,0:T(8,128)S(1)}, f32[16,64,256]{2,1,0:T(8,128)}, f32[1,1]{1,0:T(1,128)}) custom-call(f32[8,2,256,128]{3,2,1,0:T(8,128)S(1)} %shard_map.82.refs_0_), custom_call_target="tpu_custom_call" | custom-call | tf_op jit(solution)/shard_map/pallas_call | solution.py:864
  74.3 0.0 copy-start.1
  74.3 1.0 %copy.18 = f32[16,64,256]{2,1,0:T(8,128)} copy(f32[16,64,256]{2,1,0:T(8,128)S(1)} %get-tuple-element.25) | data formatting | bytes 2097152
  75.3 0.6 copy-done.1
  75.9 1.0 %copy.19 = f32[16,64,256]{2,1,0:T(8,128)} copy(f32[16,64,256]{2,1,0:T(8,128)S(1)} %copy-done.1) | data formatting | bytes 2097152
  (1 shorter events, 0.0 us)
Async XLA Ops:
  28.3 1.2 %copy-start = (f32[256,8,128]{2,1,0:T(8,128)S(1)}, f32[256,8,128]{2,1,0:T(8,128)}, u32[]{:S(2)}) copy-start(f32[256,8,128]{2,1,0:T(8,128)} %shard_map.81.blocks_ref) | copy-start | bytes 3145732
  74.3 1.6 %copy-start.1 = (f32[16,64,256]{2,1,0:T(8,128)S(1)}, f32[16,64,256]{2,1,0:T(8,128)}, u32[]{:S(2)}) copy-start(f32[16,64,256]{2,1,0:T(8,128)} %get-tuple-element.26) | copy-start | bytes 3145732

commit v4 on v3

--- a/solution.py
+++ b/solution.py
@@ -638,19 +638,25 @@
     def wait_for(ref, sem):
         pltpu.make_async_copy(ref, ref, sem).wait()
 
-    def turn(it, carry):
-        west, east = carry
+    def share(it, west, east, low, high):
         col_out[it, 0] = west
         col_out[it, 1] = east
         for dx in (-1, 1, 0):
             ask(at(dx, -1), col_out.at[it, 0], col_in.at[it, 1, 1 - dx], col_s.at[it], col_r.at[it])
             ask(at(dx, 1), col_out.at[it, 1], col_in.at[it, 0, 1 - dx], col_s.at[it], col_r.at[it])
-        row_out[it, 0] = vs[it, 1 : CZ + 1, 0, :]
-        row_out[it, 1] = vs[it, 1 : CZ + 1, CX - 1, :]
+        row_out[it, 0] = low
+        row_out[it, 1] = high
         ask(at(-1, 0), row_out.at[it, 0], row_in.at[it, 1], row_s.at[it], row_r.at[it])
         ask(at(1, 0), row_out.at[it, 1], row_in.at[it, 0], row_s.at[it], row_r.at[it])
 
+    share(0, west, east, vs[0, 1 : CZ + 1, 0, :], vs[0, 1 : CZ + 1, CX - 1, :])
+
+    zcol = lax.broadcasted_iota(jnp.int32, (CZ, LANES), 0)
+    lane_z = lax.broadcasted_iota(jnp.int32, (CZ, LANES), 1)
+
+    def turn(it, carry):
         def inner(z, c):
+            west, east = c
             halves = []
             for h in range(2):
                 cols = slice(h * LANES, (h + 1) * LANES)
@@ -666,12 +672,18 @@
             start, last = lane_half == 0, lane_half == LANES - 1
             box_left = left + jnp.where(start, 0.0, lr) + jnp.where(last, rl, ll)
             box_right = right + jnp.where(start, lr, rr) + jnp.where(last, 0.0, rl)
+            made = []
             for h, box in ((0, box_left), (1, box_right)):
                 cols = slice(h * LANES, (h + 1) * LANES)
-                vs[it + 1, z + 1, :, cols] = dg[z, :, cols] * vs[it, z + 1, :, cols] - 0.25 * box
-            return c
-
-        lax.fori_loop(0, CZ, inner, 0, unroll=4)
+                value = dg[z, :, cols] * vs[it, z + 1, :, cols] - 0.25 * box
+                vs[it + 1, z + 1, :, cols] = value
+                made.append(value)
+            for t in range(tiles_x):
+                rows = slice(8 * t, 8 * t + 8)
+                west, east = collect(z, t, made[0][rows], made[1][rows], west, east)
+            return west, east
+
+        west, east = lax.fori_loop(0, CZ, inner, (zero8, zero8), unroll=4)
 
         wait_for(row_in.at[it], row_r.at[it])
         for side, there in ((0, me_x > 0), (1, me_x < count_x - 1)):
@@ -724,8 +736,42 @@
         west_in = column(0, me_y > 0)
         east_in = column(1, me_y < count_y - 1)
 
+        @pl.when(it < ITERS - 1)
+        def _():
+            def packed(side, h, lane, first):
+                column = jnp.broadcast_to(rim[side, h, :, lane : lane + 1], (CZ, LANES))
+                return jnp.sum(jnp.where(lane_z == zcol + first, column, 0.0), axis=0, keepdims=True)
+
+            def spread(column, sub, first):
+                row = jnp.broadcast_to(column[sub : sub + 1], (CZ, LANES))
+                return jnp.sum(jnp.where(lane_z == zcol + first, row, 0.0), axis=1, keepdims=True)
+
+            final = LANES - CZ
+
+            def corners(column, fix, h, lane):
+                return (
+                    column
+                    - fix
+                    - jnp.where(sub8 == 0, packed(0, h, lane, 0), 0.0)
+                    - jnp.where(sub8 == 7, packed(1, h, lane, final), 0.0)
+                )
+
+            def row(side, sub, first):
+                near = vs[it + 1, 1 : CZ + 1, (CX - 1) * side, :]
+                left = near[:, :LANES] - jnp.where(lane_z == 0, spread(west_in, sub, first), 0.0)
+                right = near[:, LANES:] - jnp.where(lane_z == LANES - 1, spread(east_in, sub, first), 0.0)
+                return jnp.concatenate([left - rim[side, 0], right - rim[side, 1]], axis=1)
+
+            share(
+                it + 1,
+                corners(west, west_in, 0, 0),
+                corners(east, east_in, 1, LANES - 1),
+                row(0, 0, 0),
+                row(1, 7, final),
+            )
+
         def edge(z, carry):
-            west, east, cross, norm = carry
+            cross, norm = carry
             for t in range(tiles_x):
                 rows = slice(8 * t, 8 * t + 8)
                 shift = z + CZ * t
@@ -733,7 +779,6 @@
                     jnp.where(lane8 == 0, pltpu.roll(west_in, lax.rem(2 * LANES - shift, LANES), 1), 0.0),
                     jnp.where(lane8 == LANES - 1, pltpu.roll(east_in, 2 * LANES - 1 - shift - LANES, 1), 0.0),
                 ]
-                made = []
                 for h in range(2):
                     cols = slice(h * LANES, (h + 1) * LANES)
                     value = vs[it + 1, z + 1, rows, cols] - fixes[h]
@@ -744,16 +789,14 @@
                     vs[it + 1, z + 1, rows, cols] = value
                     cross = cross + value * vs[it, z + 1, rows, cols]
                     norm = norm + value * value
-                    made.append(value)
-                west, east = collect(z, t, made[0], made[1], west, east)
-            return west, east, cross, norm
-
-        west, east, cross, norm = lax.fori_loop(0, CZ, edge, (zero8, zero8, zero8, zero8), unroll=4)
+            return cross, norm
+
+        cross, norm = lax.fori_loop(0, CZ, edge, (zero8, zero8), unroll=4)
         sums[2 * it + 1] = cross
         sums[2 * it + 2] = norm
-        return west, east
-
-    lax.fori_loop(0, ITERS, turn, (west, east))
+        return carry
+
+    lax.fori_loop(0, ITERS, turn, 0)
 
     mine = zero8
     for k in range(2 * ITERS + 1):

time: 77.1 us -> 74.4 us (0.965)
  Pallas kernels: 71.7 us -> 69 us
    pallas_call x1, Pallas kernels: 36.3 us -> 33.6 us  [blend(): pl.pallas_call(kernel, out_shape=(field, field, jax.ShapeDtypeStruct((1,...]
where the time goes in v4:
time: 74.4 us; the launch traced here: 74.2 us
  Pallas kernels  69 us (93%)
  local copies, waits for them, and re-layouts  3.78 us (5%)
  between operations  1.36 us (2%)
    pallas_call x1, Pallas kernels, blend(): pl.pallas_call(kernel, out_shape=(field, field, jax.ShapeDtypeStruct((1,...  33.6 us
    pallas_call x1, Pallas kernels, route(): pl.pallas_call(kernel, out_shape=jax.ShapeDtypeStruct((slots, 8, LANES),...  27.7 us
    pallas_call x1, Pallas kernels, splat(): pl.pallas_call(splat_kernel, out_shape=jax.ShapeDtypeStruct((CX // TX, 2,...  7.72 us
    unnamed x6, local copies, waits for them, and re-layouts  3.78 us

profile of v4, /device:TPU:1, one launch (start us, length us, event | category | flops | bytes accessed | tf_op | source)
XLA Modules:
  0.0 74.2 jit_solution(16135836892528386730)
XLA Ops:
  0.6 27.7 %shard_map.81.blocks_ref = f32[256,8,128]{2,1,0:T(8,128)} custom-call(s32[128]{0:T(128)} %refs_0_.2, s32[128]{0:T(128)} %refs_1_.1, s32[1,128]{1,0:T(1,128)} %bitcast.6, f32[3,128,128]{2,1,0:T(8,128)} %bitcast.4, f32[3,128,128]{2,1,0:T(8,128)} %bitcast.5, s32[128,128]{1,0:T(8,128)} %refs_5_.1), custom_call_target="tpu_custom_call" | custom-call | tf_op jit(solution)/shard_map/pallas_call | solution.py:133
  28.3 0.0 copy-start
  28.4 1.2 %copy-done = f32[256,8,128]{2,1,0:T(8,128)S(1)} copy-done((f32[256,8,128]{2,1,0:T(8,128)S(1)}, f32[256,8,128]{2,1,0:T(8,128)}, u32[]{:S(2)}) %copy-start) | copy-done | bytes 1048600
  29.6 7.7 %shard_map.82.refs_0_ = f32[8,2,256,128]{3,2,1,0:T(8,128)S(1)} custom-call(f32[256,8,128]{2,1,0:T(8,128)S(1)} %copy-done), custom_call_target="tpu_custom_call" | custom-call | tf_op jit(solution)/shard_map/pallas_call | solution.py:260
  37.3 33.6 %shard_map.83 = (f32[16,64,256]{2,1,0:T(8,128)S(1)}, f32[16,64,256]{2,1,0:T(8,128)}, f32[1,1]{1,0:T(1,128)}) custom-call(f32[8,2,256,128]{3,2,1,0:T(8,128)S(1)} %shard_map.82.refs_0_), custom_call_target="tpu_custom_call" | custom-call | tf_op jit(solution)/shard_map/pallas_call | solution.py:907
  71.6 0.0 copy-start.1
  71.6 1.0 %copy.18 = f32[16,64,256]{2,1,0:T(8,128)} copy(f32[16,64,256]{2,1,0:T(8,128)S(1)} %get-tuple-element.25) | data formatting | bytes 2097152
  72.6 0.6 copy-done.1
  73.2 1.0 %copy.19 = f32[16,64,256]{2,1,0:T(8,128)} copy(f32[16,64,256]{2,1,0:T(8,128)S(1)} %copy-done.1) | data formatting | bytes 2097152
  (1 shorter events, 0.0 us)
Async XLA Ops:
  28.3 1.2 %copy-start = (f32[256,8,128]{2,1,0:T(8,128)S(1)}, f32[256,8,128]{2,1,0:T(8,128)}, u32[]{:S(2)}) copy-start(f32[256,8,128]{2,1,0:T(8,128)} %shard_map.81.blocks_ref) | copy-start | bytes 3145732
  71.6 1.6 %copy-start.1 = (f32[16,64,256]{2,1,0:T(8,128)S(1)}, f32[16,64,256]{2,1,0:T(8,128)}, u32[]{:S(2)}) copy-start(f32[16,64,256]{2,1,0:T(8,128)} %get-tuple-element.26) | copy-start | bytes 3145732

commit v5 on v4

--- a/solution.py
+++ b/solution.py
@@ -13,8 +13,9 @@
 POINTS = 128
 ITERS = 3
 LANES = 128
-GROUP = 32
+GROUP = 64
 SHIFT = 6.5
+STRIDE = 37
 TRUST = 100.0
 
 screen_weight = 4.0
@@ -47,7 +48,7 @@
     me = lax.axis_index("gx") * count_y + lax.axis_index("gy")
 
     def place(d):
-        flat = lax.rem(me + d, devices)
+        flat = lax.rem(me + lax.rem(d * STRIDE, devices), devices)
         return flat, (flat // count_y, lax.rem(flat, count_y))
 
     barrier = pltpu.get_barrier_semaphore()
@@ -86,7 +87,7 @@
 
     lane = lax.broadcasted_iota(jnp.int32, (1, LANES), 1)
 
-    def fill(o, carry):
+    def fill(o):
         for c in range(2):
             k = jnp.minimum(jnp.maximum(index_s[c, o], 0), blocks - 1)
             there = index_s[2 + c, o]
@@ -97,17 +98,12 @@
             send[slot, 6:7, :] = cell_ref[pl.ds(k, 1), :].astype(jnp.float32)
             header = jnp.where(lane == 0, tile_ref[k], jnp.where(lane == 1, count_ref[k] * there, 0))
             send[slot, 7:8, :] = header.astype(jnp.float32)
-        return carry
-
-    lax.fori_loop(0, devices, fill, 0, unroll=4)
-    keep = pltpu.make_async_copy(
-        send.at[pl.ds(2 * me, 2)], out_ref.at[pl.ds(2 * me, 2)], copy_sem
-    )
-    keep.start()
+
     pl.semaphore_wait(barrier, devices - 1)
 
     def ship(d, carry):
         flat, target = place(d)
+        fill(flat)
         pltpu.make_async_remote_copy(
             src_ref=send.at[pl.ds(2 * flat, 2)],
             dst_ref=out_ref.at[pl.ds(2 * me, 2)],
@@ -117,6 +113,11 @@
         return carry
 
     lax.fori_loop(1, devices, ship, 0)
+    fill(me)
+    keep = pltpu.make_async_copy(
+        send.at[pl.ds(2 * me, 2)], out_ref.at[pl.ds(2 * me, 2)], copy_sem
+    )
+    keep.start()
     keep.wait()
     most = pl.ds(0, 2 * (devices - 1))
     pltpu.make_async_copy(out_ref.at[most], out_ref.at[most], recv_sem).wait()

time: 74.4 us -> 73.5 us (0.988)
  Pallas kernels: 69 us -> 68.1 us
    pallas_call x1, Pallas kernels: 7.72 us -> 12.8 us  [splat(): pl.pallas_call(splat_kernel, out_shape=jax.ShapeDtypeStruct((CX // TX, 2,...]
    pallas_call x1, Pallas kernels: 33.6 us -> 29 us  [blend(): pl.pallas_call(kernel, out_shape=(field, field, jax.ShapeDtypeStruct((1,...]
    pallas_call x1, Pallas kernels: 27.7 us -> 26.4 us  [route(): pl.pallas_call(kernel, out_shape=jax.ShapeDtypeStruct((slots, 8, LANES),...]
where the time goes in v5:
time: 73.5 us; the launch traced here: 73.3 us
  Pallas kernels  68.1 us (93%)
  local copies, waits for them, and re-layouts  3.78 us (5%)
  between operations  1.36 us (2%)
    pallas_call x1, Pallas kernels, blend(): pl.pallas_call(kernel, out_shape=(field, field, jax.ShapeDtypeStruct((1,...  29 us
    pallas_call x1, Pallas kernels, route(): pl.pallas_call(kernel, out_shape=jax.ShapeDtypeStruct((slots, 8, LANES),...  26.4 us
    pallas_call x1, Pallas kernels, splat(): pl.pallas_call(splat_kernel, out_shape=jax.ShapeDtypeStruct((CX // TX, 2,...  12.8 us
    unnamed x6, local copies, waits for them, and re-layouts  3.78 us

profile of v5, /device:TPU:1, one launch (start us, length us, event | category | flops | bytes accessed | tf_op | source)
XLA Modules:
  0.0 73.3 jit_solution(7158643459000508190)
XLA Ops:
  0.6 26.4 %shard_map.81.blocks_ref = f32[256,8,128]{2,1,0:T(8,128)} custom-call(s32[128]{0:T(128)} %refs_0_.2, s32[128]{0:T(128)} %refs_1_.1, s32[1,128]{1,0:T(1,128)} %bitcast.6, f32[3,128,128]{2,1,0:T(8,128)} %bitcast.4, f32[3,128,128]{2,1,0:T(8,128)} %bitcast.5, s32[128,128]{1,0:T(8,128)} %refs_5_.1), custom_call_target="tpu_custom_call" | custom-call | tf_op jit(solution)/shard_map/pallas_call | solution.py:134
  27.0 0.0 copy-start
  27.0 1.2 %copy-done = f32[256,8,128]{2,1,0:T(8,128)S(1)} copy-done((f32[256,8,128]{2,1,0:T(8,128)S(1)}, f32[256,8,128]{2,1,0:T(8,128)}, u32[]{:S(2)}) %copy-start) | copy-done | bytes 1048600
  28.2 12.8 %shard_map.82.refs_0_ = f32[8,2,256,128]{3,2,1,0:T(8,128)S(1)} custom-call(f32[256,8,128]{2,1,0:T(8,128)S(1)} %copy-done), custom_call_target="tpu_custom_call" | custom-call | tf_op jit(solution)/shard_map/pallas_call | solution.py:261
  41.0 29.0 %shard_map.83 = (f32[16,64,256]{2,1,0:T(8,128)S(1)}, f32[16,64,256]{2,1,0:T(8,128)}, f32[1,1]{1,0:T(1,128)}) custom-call(f32[8,2,256,128]{3,2,1,0:T(8,128)S(1)} %shard_map.82.refs_0_), custom_call_target="tpu_custom_call" | custom-call | tf_op jit(solution)/shard_map/pallas_call | solution.py:908
  70.7 0.0 copy-start.1
  70.7 1.0 %copy.18 = f32[16,64,256]{2,1,0:T(8,128)} copy(f32[16,64,256]{2,1,0:T(8,128)S(1)} %get-tuple-element.25) | data formatting | bytes 2097152
  71.7 0.6 copy-done.1
  72.3 1.0 %copy.19 = f32[16,64,256]{2,1,0:T(8,128)} copy(f32[16,64,256]{2,1,0:T(8,128)S(1)} %copy-done.1) | data formatting | bytes 2097152
  (1 shorter events, 0.0 us)
Async XLA Ops:
  27.0 1.2 %copy-start = (f32[256,8,128]{2,1,0:T(8,128)S(1)}, f32[256,8,128]{2,1,0:T(8,128)}, u32[]{:S(2)}) copy-start(f32[256,8,128]{2,1,0:T(8,128)} %shard_map.81.blocks_ref) | copy-start | bytes 3145732
  70.7 1.6 %copy-start.1 = (f32[16,64,256]{2,1,0:T(8,128)S(1)}, f32[16,64,256]{2,1,0:T(8,128)}, u32[]{:S(2)}) copy-start(f32[16,64,256]{2,1,0:T(8,128)} %get-tuple-element.26) | copy-start | bytes 3145732

commit v6 on v5

--- a/solution.py
+++ b/solution.py
@@ -270,7 +270,7 @@
             pltpu.SMEM((slots + GROUP,), jnp.int32),
             pltpu.SemaphoreType.DMA,
         ],
-        compiler_params=pltpu.CompilerParams(vmem_limit_bytes=24 << 20),
+        compiler_params=pltpu.CompilerParams(vmem_limit_bytes=58 << 20),
     )(blocks)
 
 
@@ -608,7 +608,7 @@
         dg[:, rows, :] = (6.75 - SHIFT) + screen_weight * acc_ref[t, 1].T.reshape(CZ, TX, CY)
         return carry
 
-    lax.fori_loop(0, tiles_x, unfold, 0)
+    lax.fori_loop(0, tiles_x, unfold, 0, unroll=4)
 
     def collect(z, t, left, right, west, east):
         shift = z + CZ * t

time: 73.5 us -> 73.2 us (level)
  Pallas kernels: 68.1 us -> 69.9 us
  local copies, waits for them, and re-layouts: 3.78 us -> 2.57 us
    pallas_call x1, Pallas kernels: 29 us -> 35 us  [blend(): pl.pallas_call(kernel, out_shape=(field, field, jax.ShapeDtypeStruct((1,...]
    pallas_call x1, Pallas kernels: 12.8 us -> 8.47 us  [splat(): pl.pallas_call(splat_kernel, out_shape=jax.ShapeDtypeStruct((CX // TX, 2,...]
    unnamed x6 -> x4, local copies, waits for them, and re-layouts: 3.78 us -> 2.57 us
where the time goes in v6:
time: 73.2 us; the launch traced here: 73.7 us
  Pallas kernels  69.9 us (95%)
  local copies, waits for them, and re-layouts  2.57 us (4%)
  between operations  1.24 us (2%)
    pallas_call x1, Pallas kernels, blend(): pl.pallas_call(kernel, out_shape=(field, field, jax.ShapeDtypeStruct((1,...  35 us
    pallas_call x1, Pallas kernels, route(): pl.pallas_call(kernel, out_shape=jax.ShapeDtypeStruct((slots, 8, LANES),...  26.4 us
    pallas_call x1, Pallas kernels, splat(): pl.pallas_call(splat_kernel, out_shape=jax.ShapeDtypeStruct((CX // TX, 2,...  8.47 us
    unnamed x4, local copies, waits for them, and re-layouts  2.57 us

profile of v6, /device:TPU:1, one launch (start us, length us, event | category | flops | bytes accessed | tf_op | source)
XLA Modules:
  0.0 73.7 jit_solution(10773378985208761761)
XLA Ops:
  0.6 26.4 %shard_map.81.blocks_ref = f32[256,8,128]{2,1,0:T(8,128)} custom-call(s32[128]{0:T(128)} %refs_0_.2, s32[128]{0:T(128)} %refs_1_.1, s32[1,128]{1,0:T(1,128)} %bitcast.6, f32[3,128,128]{2,1,0:T(8,128)} %bitcast.4, f32[3,128,128]{2,1,0:T(8,128)} %bitcast.5, s32[128,128]{1,0:T(8,128)} %refs_5_.1), custom_call_target="tpu_custom_call" | custom-call | tf_op jit(solution)/shard_map/pallas_call | solution.py:134
  27.0 8.5 %shard_map.82.refs_0_ = f32[8,2,256,128]{3,2,1,0:T(8,128)S(1)} custom-call(f32[256,8,128]{2,1,0:T(8,128)} %shard_map.81.blocks_ref), custom_call_target="tpu_custom_call" | custom-call | tf_op jit(solution)/shard_map/pallas_call | solution.py:261
  35.5 35.0 %shard_map.83 = (f32[16,64,256]{2,1,0:T(8,128)S(1)}, f32[16,64,256]{2,1,0:T(8,128)}, f32[1,1]{1,0:T(1,128)}) custom-call(f32[8,2,256,128]{3,2,1,0:T(8,128)S(1)} %shard_map.82.refs_0_), custom_call_target="tpu_custom_call" | custom-call | tf_op jit(solution)/shard_map/pallas_call | solution.py:908
  71.1 0.0 copy-start
  71.1 1.0 %copy.18 = f32[16,64,256]{2,1,0:T(8,128)} copy(f32[16,64,256]{2,1,0:T(8,128)S(1)} %get-tuple-element.25) | data formatting | bytes 2097152
  72.1 0.6 copy-done
  72.7 1.0 %copy.19 = f32[16,64,256]{2,1,0:T(8,128)} copy(f32[16,64,256]{2,1,0:T(8,128)S(1)} %copy-done) | data formatting | bytes 2097152
  (1 shorter events, 0.0 us)
Async XLA Ops:
  71.1 1.6 %copy-start = (f32[16,64,256]{2,1,0:T(8,128)S(1)}, f32[16,64,256]{2,1,0:T(8,128)}, u32[]{:S(2)}) copy-start(f32[16,64,256]{2,1,0:T(8,128)} %get-tuple-element.26) | copy-start | bytes 3145732
